TPU v7x, 128 devices: a whole 4x4x4 slice. The times are simulated.
128 devices in a mesh: dp: 8 (over x, core), ctx: 16 (over y, z).
Axes of the slice: x: 4, y: 4, z: 4, core: 2. Of those that a mesh axis runs over, the one named last changes fastest.
Arguments:
- mixed_in: bfloat16 [8, 2048, 4096], P('dp', 'ctx'), may hold values from -6 to 6
- conv_weight: float32 [4, 4096], replicated, may hold values from -3 to 3
- gate_in: float32 [8, 2048, 32], P('dp', 'ctx'), may hold values from -9.7 to 9
- head_params: float32 [2, 16], replicated, may hold values from -3.5 to 1
- doc_lengths: int32 [8, 8], P('dp'), may hold values from 1 to 1024, 2048 in all within a row
- d_core: bfloat16 [8, 2048, 2048], P('dp', 'ctx'), may hold values from -6 to 6
Outputs:
- core_out: bfloat16 [8, 2048, 2048], P('dp', 'ctx')
- d_mixed: bfloat16 [8, 2048, 4096], P('dp', 'ctx')
- d_gates: float32 [8, 2048, 32], P('dp', 'ctx')
- d_conv: float32 [4, 4096], replicated
- d_head: float32 [2, 16], replicated
Inputs may be any that keep to these rules, and one draw needn't show every extreme that they name: `doc_lengths`: the longest of a stream's 8 documents has exactly 1024 tokens.
All inputs are finite; a program needn't handle non-finite values.
Results may differ from a plain program's by a relative error of at most 0.0095.
Values may be sent and summed in bfloat16 or wider, within the bound.
A program may use at most 256 MiB of HBM per device.

v0:
```python
import jax
import jax.numpy as jnp
from jax import lax
from jax.sharding import PartitionSpec as P

VALUE_HEADS = 16
QK_HEADS = 8
DK = 128
DV = 128
GROUP = 64


def shifted(value, axis, steps):
    count = lax.axis_size(axis)
    initial, last = (max(0, -steps), min(count, count - steps))
    return lax.ppermute(value, axis, [(source, source + steps) for source in range(initial, last)])


def group_head(memory, queries, key_rows, value_rows, decays, beta_rows, doc_ids, doc_before):
    highest = lax.Precision.HIGHEST
    length = queries.shape[0]
    summed = jnp.cumsum(decays)
    row_idx = jnp.arange(length)[:, None]
    col_idx = jnp.arange(length)[None, :]
    linked = (doc_ids[:, None] == doc_ids[None, :]) & (row_idx >= col_idx)
    spans = jnp.where(linked, jnp.exp(jnp.minimum(summed[:, None] - summed[None, :], 0.0)), 0.0)
    carried = jnp.exp(summed) * (doc_ids == doc_before).astype(jnp.float32)
    key_prod = jnp.dot(key_rows, key_rows.T, precision=highest)
    strict = jnp.where(row_idx > col_idx, beta_rows[:, None] * spans * key_prod, 0.0)
    system = strict + jnp.eye(length, dtype=jnp.float32)
    right_side = beta_rows[:, None] * value_rows - (beta_rows * carried)[:, None] * jnp.dot(
        key_rows, memory.T, precision=highest
    )
    updates = lax.linalg.triangular_solve(
        system, right_side, left_side=True, lower=True, unit_diagonal=True
    )
    scores = spans * jnp.dot(queries, key_rows.T, precision=highest)
    outputs = carried[:, None] * jnp.dot(queries, memory.T, precision=highest) + jnp.dot(
        scores, updates, precision=highest
    )
    memory_new = carried[-1] * memory + jnp.dot(
        (spans[-1][:, None] * updates).T, key_rows, precision=highest
    )
    return (memory_new, outputs)


def delta_core(queries, key_rows, value_rows, decays, beta_rows, doc_ext, memory):
    length = queries.shape[0]
    blocks = length // GROUP
    doc_ids = doc_ext[1:].reshape(blocks, GROUP)
    doc_before = doc_ext[:-1].reshape(blocks, GROUP)[:, 0]

    def folded(array):
        return array.reshape((blocks, GROUP) + array.shape[1:])

    per_head = jax.vmap(group_head, in_axes=(0, 1, 1, 1, 1, 1, None, None), out_axes=(0, 1))

    def advance(carry_state, inputs):
        return per_head(carry_state, *inputs)

    final, outputs = lax.scan(
        jax.checkpoint(advance),
        memory,
        (
            folded(queries),
            folded(key_rows),
            folded(value_rows),
            folded(decays),
            folded(beta_rows),
            doc_ids,
            doc_before,
        ),
    )
    return (outputs.reshape((length,) + outputs.shape[2:]), final)


def prepare(x_ext, conv_w, gates, head_params, doc_all):
    taps = conv_w.shape[0]
    length = x_ext.shape[0] - taps + 1
    mixed = jnp.zeros((length, x_ext.shape[1]), jnp.float32)
    for offset in range(taps):
        linked = (doc_all[offset : offset + length] == doc_all[taps - 1 :]).astype(jnp.float32)
        mixed = mixed + x_ext[offset : offset + length] * conv_w[offset] * linked[:, None]
    mixed = jax.nn.silu(mixed)
    width_qk = QK_HEADS * DK
    queries = mixed[:, :width_qk].reshape(length, QK_HEADS, DK)
    key_rows = mixed[:, width_qk : 2 * width_qk].reshape(length, QK_HEADS, DK)
    value_rows = mixed[:, 2 * width_qk :].reshape(length, VALUE_HEADS, DV)
    queries = (
        queries
        * lax.rsqrt(jnp.sum(queries * queries, axis=-1, keepdims=True) + 1e-06)
        * DK ** (-0.5)
    )
    key_rows = key_rows * lax.rsqrt(jnp.sum(key_rows * key_rows, axis=-1, keepdims=True) + 1e-06)
    ratio = VALUE_HEADS // QK_HEADS
    queries = jnp.repeat(queries, ratio, axis=1)
    key_rows = jnp.repeat(key_rows, ratio, axis=1)
    decays = -jnp.exp(head_params[0]) * jax.nn.softplus(gates[:, :VALUE_HEADS] + head_params[1])
    beta_rows = jax.nn.sigmoid(gates[:, VALUE_HEADS:])
    return (queries, key_rows, value_rows, decays, beta_rows)


def on_device(mixed_in, conv_weight, gate_in, head_params, doc_lengths, d_core):
    highest = lax.Precision.HIGHEST
    rows = mixed_in.shape[1]
    taps = conv_weight.shape[0]
    first_pos = lax.axis_index("ctx") * rows
    tail_rows = shifted(mixed_in[0, rows - taps + 1 :], "ctx", 1)
    x_ext = jnp.concatenate([tail_rows, mixed_in[0]], axis=0).astype(jnp.float32)
    ends = jnp.cumsum(doc_lengths[0])
    positions = first_pos + jnp.arange(rows + taps - 1, dtype=jnp.int32) - (taps - 1)
    doc_all = jnp.sum((ends[None, :] <= positions[:, None]).astype(jnp.int32), axis=1)
    doc_ext = doc_all[taps - 2 :]
    identity = jnp.broadcast_to(jnp.eye(DK, dtype=jnp.float32), (VALUE_HEADS, DK, DK))
    empty_state = jnp.zeros((VALUE_HEADS, DV, DK), jnp.float32)
    start_ext = jnp.concatenate([empty_state, identity], axis=1)

    def local_pass(x_local, conv_w, gates, params):
        queries, key_rows, value_rows, decays, beta_rows = prepare(
            x_local, conv_w, gates, params, doc_all
        )
        value_ext = jnp.concatenate(
            [value_rows, jnp.zeros((rows, VALUE_HEADS, DK), jnp.float32)], axis=2
        )
        return delta_core(queries, key_rows, value_ext, decays, beta_rows, doc_ext, start_ext)

    (ext_out, end_state), pullback = jax.vjp(
        local_pass, x_ext, conv_weight, gate_in[0], head_params
    )
    out_local = ext_out[:, :, :DV]
    carry_out = ext_out[:, :, DV:]
    offset_part = end_state[:, :DV]
    transition = end_state[:, DV:]
    transposed = jnp.swapaxes(transition, 1, 2)
    grad_out = d_core[0].astype(jnp.float32).reshape(rows, VALUE_HEADS, DV)
    grad_local = jnp.einsum("thv,thk->hvk", grad_out, carry_out, precision=highest)
    length_ctx = lax.axis_size("ctx")

    def forward_turn(index_i, incoming):
        leaving = jnp.einsum("hvk,hkj->hvj", incoming, transition, precision=highest) + offset_part
        return shifted(leaving, "ctx", 1)

    state_start = lax.fori_loop(0, length_ctx - 1, forward_turn, empty_state)

    def backward_turn(index_i, incoming):
        leaving = jnp.einsum("hvk,hkj->hvj", incoming, transposed, precision=highest) + grad_local
        return shifted(leaving.astype(jnp.bfloat16), "ctx", -1).astype(leaving.dtype)

    grad_end = lax.fori_loop(0, length_ctx - 1, backward_turn, empty_state)
    outputs = out_local + jnp.einsum("thk,hvk->thv", carry_out, state_start, precision=highest)
    core_out = outputs.reshape(1, rows, VALUE_HEADS * DV).astype(jnp.bfloat16)
    grad_ext = jnp.concatenate(
        [grad_out, jnp.einsum("thv,hvk->thk", grad_out, state_start, precision=highest)], axis=2
    )
    grad_state = jnp.concatenate(
        [grad_end, jnp.einsum("hvk,hvj->hkj", state_start, grad_end, precision=highest)], axis=1
    )
    grad_x, grad_conv, grad_gates, grad_params = pullback((grad_ext, grad_state))
    back_tail = shifted(grad_x[: taps - 1].astype(jnp.bfloat16), "ctx", -1).astype(jnp.float32)
    grad_rows = grad_x[taps - 1 :]
    grad_rows = jnp.concatenate(
        [grad_rows[: rows - taps + 1], grad_rows[rows - taps + 1 :] + back_tail], axis=0
    )
    d_mixed = grad_rows.astype(jnp.bfloat16)[None]
    d_conv, d_head = lax.psum((grad_conv, grad_params), ("dp", "ctx"))
    return (core_out, d_mixed, grad_gates[None], d_conv, d_head)


def solution(mesh):
    return jax.shard_map(
        on_device,
        mesh=mesh,
        in_specs=(
            P("dp", "ctx", None),
            P(),
            P("dp", "ctx", None),
            P(),
            P("dp", None),
            P("dp", "ctx", None),
        ),
        out_specs=(P("dp", "ctx", None), P("dp", "ctx", None), P("dp", "ctx", None), P(), P()),
        check_vma=False,
    )
```

profile of v0, /device:TPU:1, one launch (start us, length us, event | category | flops | bytes accessed | tf_op | source)
XLA Modules:
  0.0 1512.0 jit_solution(15754789417390678872)
XLA Ops:
  42.3 198.5 %while.64 = (s32[]{:T(128)}, f32[16,256,128]{2,1,0:T(8,128)S(1)}, f32[2,64,16,256]{3,1,0,2:T(8,128)}, f32[2,16,256,128]{3,2,1,0:T(8,128)}, f32[2,64,16]{2,1,0:T(...) while((s32[]{:T(128)}, f32[16,256,128]{2,1,0:T(8,128)S(1)}, ...), condition=%wide.region_6.8_spmd.clone, body=%wide.region_4.7_spmd.clone.sunk | while | flops 1815709952 | bytes 91543808 | solution.py:61
  46.6 80.0 %custom-call.23 = f32[16,1,64,64]{2,3,1,0:T(8,128)} custom-call(f32[16,1,64,64]{3,2,1,0:T(8,128)} %fusion.366), custom_call_target="InvertDiagBlocksLowerTriangular" | custom-call | tf_op jit(solution)/shard_map/jvp()/while/body/eval_jaxpr/vmap()/triangular_solve/custom-call.1 | solution.py:34
  145.5 80.0 %custom-call.23 = f32[16,1,64,64]{2,3,1,0:T(8,128)} custom-call(f32[16,1,64,64]{3,2,1,0:T(8,128)} %fusion.366), custom_call_target="InvertDiagBlocksLowerTriangular" | custom-call | tf_op jit(solution)/shard_map/jvp()/while/body/eval_jaxpr/vmap()/triangular_solve/custom-call.1 | solution.py:34
  251.0 373.3 %while.62 = (s32[]{:T(128)}, f32[16,128,128]{2,1,0:T(8,128)S(1)}, f32[16,128,128]{2,1,0:T(8,128)}, f32[16,128,128]{2,1,0:T(8,128)S(1)}, s32[]{:T(128)}) while((s32[]{:T(128)}, f32[16,128,128]{2,1,0:T(8,128)S(1)}, f32[16,128,128]{2,1,0:T(8,128)}, f32[16,128,128]{2,1,0:T(8,128)S(1)}, s32[]{:T(128)}) %tuple.236), condition=%wide.region_8.10_spmd, body=%wide.region_7.9_spmd.sunk | while | flops 402915328 | bytes 8388709 | solution.py:143
  258.0 21.7 %collective-permute-done = f32[16,128,128]{2,1,0:T(8,128)S(1)} collective-permute-done((f32[16,128,128]{2,1,0:T(8,128)}, f32[16,128,128]{2,1,0:T(8,128)S(1)}, u32[]{:S(2)}, u32[]{:S(2)}) %collective-permute-start) | collective-permute-done | bytes 1048608 | tf_op jit(solution)/shard_map/while/body/eval_jaxpr/ppermute | solution.py:16
  287.1 20.8 %collective-permute-done = f32[16,128,128]{2,1,0:T(8,128)S(1)} collective-permute-done((f32[16,128,128]{2,1,0:T(8,128)}, f32[16,128,128]{2,1,0:T(8,128)S(1)}, u32[]{:S(2)}, u32[]{:S(2)}) %collective-permute-start) | collective-permute-done | bytes 1048608 | tf_op jit(solution)/shard_map/while/body/eval_jaxpr/ppermute | solution.py:16
  315.3 19.9 %collective-permute-done = f32[16,128,128]{2,1,0:T(8,128)S(1)} collective-permute-done((f32[16,128,128]{2,1,0:T(8,128)}, f32[16,128,128]{2,1,0:T(8,128)S(1)}, u32[]{:S(2)}, u32[]{:S(2)}) %collective-permute-start) | collective-permute-done | bytes 1048608 | tf_op jit(solution)/shard_map/while/body/eval_jaxpr/ppermute | solution.py:16
  342.6 19.0 %collective-permute-done = f32[16,128,128]{2,1,0:T(8,128)S(1)} collective-permute-done((f32[16,128,128]{2,1,0:T(8,128)}, f32[16,128,128]{2,1,0:T(8,128)S(1)}, u32[]{:S(2)}, u32[]{:S(2)}) %collective-permute-start) | collective-permute-done | bytes 1048608 | tf_op jit(solution)/shard_map/while/body/eval_jaxpr/ppermute | solution.py:16
  369.0 18.0 %collective-permute-done = f32[16,128,128]{2,1,0:T(8,128)S(1)} collective-permute-done((f32[16,128,128]{2,1,0:T(8,128)}, f32[16,128,128]{2,1,0:T(8,128)S(1)}, u32[]{:S(2)}, u32[]{:S(2)}) %collective-permute-start) | collective-permute-done | bytes 1048608 | tf_op jit(solution)/shard_map/while/body/eval_jaxpr/ppermute | solution.py:16
  395.4 17.1 %collective-permute-done = f32[16,128,128]{2,1,0:T(8,128)S(1)} collective-permute-done((f32[16,128,128]{2,1,0:T(8,128)}, f32[16,128,128]{2,1,0:T(8,128)S(1)}, u32[]{:S(2)}, u32[]{:S(2)}) %collective-permute-start) | collective-permute-done | bytes 1048608 | tf_op jit(solution)/shard_map/while/body/eval_jaxpr/ppermute | solution.py:16
  422.0 16.2 %collective-permute-done = f32[16,128,128]{2,1,0:T(8,128)S(1)} collective-permute-done((f32[16,128,128]{2,1,0:T(8,128)}, f32[16,128,128]{2,1,0:T(8,128)S(1)}, u32[]{:S(2)}, u32[]{:S(2)}) %collective-permute-start) | collective-permute-done | bytes 1048608 | tf_op jit(solution)/shard_map/while/body/eval_jaxpr/ppermute | solution.py:16
  441.6 6.2 collective-permute-start
  447.8 15.3 %collective-permute-done = f32[16,128,128]{2,1,0:T(8,128)S(1)} collective-permute-done((f32[16,128,128]{2,1,0:T(8,128)}, f32[16,128,128]{2,1,0:T(8,128)S(1)}, u32[]{:S(2)}, u32[]{:S(2)}) %collective-permute-start) | collective-permute-done | bytes 1048608 | tf_op jit(solution)/shard_map/while/body/eval_jaxpr/ppermute | solution.py:16
  466.4 6.2 collective-permute-start
  472.6 14.4 collective-permute-done
  490.3 6.2 collective-permute-start
  496.5 13.4 collective-permute-done
  513.2 6.2 collective-permute-start
  519.4 12.5 collective-permute-done
  535.3 6.2 collective-permute-start
  541.5 12.4 collective-permute-done
  557.2 6.2 collective-permute-start
  563.4 13.2 collective-permute-done
  579.9 6.2 collective-permute-start
  586.1 14.0 collective-permute-done
  609.6 14.8 collective-permute-done
  633.3 284.8 %while.65 = (s32[]{:T(128)}, f32[16,128,128]{2,1,0:T(8,128)S(1)}, f32[16,128,128]{2,1,0:T(8,128)}, f32[16,128,128]{2,1,0:T(8,128)}, s32[]{:T(128)}, /*index=5*/s32[]{:T(128)}) while((s32[]{:T(128)}, f32[16,128,128]{2,1,0:T(8,128)S(1)}, f32[16,128,128]{2,1,0:T(8,128)}, f32[16,128,128]{2,1,0:T(8,128)}, s32[]{:T(128)}, ...), condition=%wide.region_10.12_spmd.clone, body=%wide.region_9.11_spmd.clone.sunk | while | flops 403701760 | bytes 7340151 | solution.py:149
  638.1 12.3 collective-permute-done.1
  656.4 14.9 collective-permute-done.1
  677.3 16.0 %collective-permute-done.1 = bf16[16,128,128]{2,1,0:T(8,128)(2,1)} collective-permute-done((bf16[16,128,128]{2,1,0:T(8,128)(2,1)}, bf16[16,128,128]{2,1,0:T(8,128)(2,1)}, u32[]{:S(2)}, u32[]{:S(2)}) %collective-permute-start.1) | collective-permute-done | bytes 524320 | tf_op jit(solution)/shard_map/while/body/eval_jaxpr/ppermute | solution.py:16
  699.3 17.1 %collective-permute-done.1 = bf16[16,128,128]{2,1,0:T(8,128)(2,1)} collective-permute-done((bf16[16,128,128]{2,1,0:T(8,128)(2,1)}, bf16[16,128,128]{2,1,0:T(8,128)(2,1)}, u32[]{:S(2)}, u32[]{:S(2)}) %collective-permute-start.1) | collective-permute-done | bytes 524320 | tf_op jit(solution)/shard_map/while/body/eval_jaxpr/ppermute | solution.py:16
  722.4 17.9 %collective-permute-done.1 = bf16[16,128,128]{2,1,0:T(8,128)(2,1)} collective-permute-done((bf16[16,128,128]{2,1,0:T(8,128)(2,1)}, bf16[16,128,128]{2,1,0:T(8,128)(2,1)}, u32[]{:S(2)}, u32[]{:S(2)}) %collective-permute-start.1) | collective-permute-done | bytes 524320 | tf_op jit(solution)/shard_map/while/body/eval_jaxpr/ppermute | solution.py:16
  746.3 15.0 collective-permute-done.1
  767.3 13.2 collective-permute-done.1
  786.5 12.4 collective-permute-done.1
  804.9 11.5 collective-permute-done.1
  822.4 10.6 collective-permute-done.1
  839.0 10.1 collective-permute-done.1
  855.1 10.8 collective-permute-done.1
  871.8 11.1 collective-permute-done.1
  888.9 11.1 collective-permute-done.1
  905.9 11.1 collective-permute-done.1
  926.8 303.2 %while.63 = (s32[]{:T(128)}, f32[16,256,128]{2,1,0:T(8,128)}, f32[2,64,16,128]{3,1,0,2:T(8,128)}, f32[2,64,16,128]{3,1,0,2:T(8,128)}, f32[2,64,16,256]{3,2,1,0:T...) while((s32[]{:T(128)}, f32[16,256,128]{2,1,0:T(8,128)}, ...), condition=%wide.region_22.24_spmd, body=%wide.region_11.23_spmd.sunk | while | flops 4894860288 | bytes 205434480 | solution.py:61
  967.3 80.0 %custom-call.22 = f32[16,1,64,64]{2,3,1,0:T(8,128)} custom-call(f32[16,1,64,64]{3,2,1,0:T(8,128)} %get-tuple-element.1358), custom_call_target="InvertDiagBlocksLowerTriangular" | custom-call | tf_op jit(solution)/shard_map/transpose(jvp())/while/body/eval_jaxpr/checkpoint/vmap()/triangular_solve | solution.py:34
  1103.2 80.0 %custom-call.22 = f32[16,1,64,64]{2,3,1,0:T(8,128)} custom-call(f32[16,1,64,64]{3,2,1,0:T(8,128)} %get-tuple-element.1358), custom_call_target="InvertDiagBlocksLowerTriangular" | custom-call | tf_op jit(solution)/shard_map/transpose(jvp())/while/body/eval_jaxpr/checkpoint/vmap()/triangular_solve | solution.py:34
  1241.5 9.0 multiply_reduce_fusion.6
  1262.2 105.7 %psum.15 = f32[2,16]{1,0:T(2,128)} all-reduce(f32[2,16]{1,0:T(2,128)S(1)} %pad_add_fusion.2), channel_id=1, replica_groups=mesh['dp'=8,'ctx'=16] {'dp','ctx'}, use_global_device_ids=true, to_apply=%region_34.36 | all-reduce | flops 32 | bytes 256 | tf_op jit(solution)/shard_map/psum | solution.py:165
  1373.3 130.2 %all-reduce.21.cloned.1.call-done = f32[4,4096]{1,0:T(4,128)} async-done(((f32[4,4096]{1,0:T(4,128)}), f32[4,4096]{1,0:T(4,128)}) %all-reduce.21.cloned.1.call-update) | async-done | bytes 65552 | tf_op jit(solution)/shard_map/psum | solution.py:165
  (529 shorter events, 417.2 us)
Async XLA Ops:
  7.2 10.6 copy-start.48
  7.2 12.1 copy-start.43
  7.2 1496.3 %all-reduce.21.cloned.1.call-start = ((), (), s32[]{:S(2)}) async-start(), calls=%async_computation | async-start | bytes 131072 | tf_op jit(solution)/shard_map/psum | solution.py:165
  8.2 13.6 collective-permute-start.2
  13.7 11.5 copy-start.65
  13.7 11.5 copy-start.67
  13.7 11.5 copy-start.69
  15.6 9.6 copy-start.49
  15.6 9.6 copy-start.51
  15.6 9.6 copy-start.53
  15.7 9.6 copy-start.55
  32.8 9.1 copy-start.58
  254.4 25.3 %collective-permute-start = (f32[16,128,128]{2,1,0:T(8,128)}, f32[16,128,128]{2,1,0:T(8,128)S(1)}, u32[]{:S(2)}, u32[]{:S(2)}) collective-permute-start(f32[16,128,128]{2,1,0:T(8,128)} %convolution_add_fusion.6), channel_id=1, source_target_pairs={{0,1},{1,2},{2,3},{3,4},{4,5},{5,6},{6,7},{7,8},{8,9},{9,10},{10,1... | collective-permute-start | bytes 3145736 | tf_op jit(solution)/shard_map/while/body/eval_jaxpr/ppermute | solution.py:16
  283.0 24.9 %collective-permute-start = (f32[16,128,128]{2,1,0:T(8,128)}, f32[16,128,128]{2,1,0:T(8,128)S(1)}, u32[]{:S(2)}, u32[]{:S(2)}) collective-permute-start(f32[16,128,128]{2,1,0:T(8,128)} %convolution_add_fusion.6), channel_id=1, source_target_pairs={{0,1},{1,2},{2,3},{3,4},{4,5},{5,6},{6,7},{7,8},{8,9},{9,10},{10,1... | collective-permute-start | bytes 3145736 | tf_op jit(solution)/shard_map/while/body/eval_jaxpr/ppermute | solution.py:16
  311.2 23.9 %collective-permute-start = (f32[16,128,128]{2,1,0:T(8,128)}, f32[16,128,128]{2,1,0:T(8,128)S(1)}, u32[]{:S(2)}, u32[]{:S(2)}) collective-permute-start(f32[16,128,128]{2,1,0:T(8,128)} %convolution_add_fusion.6), channel_id=1, source_target_pairs={{0,1},{1,2},{2,3},{3,4},{4,5},{5,6},{6,7},{7,8},{8,9},{9,10},{10,1... | collective-permute-start | bytes 3145736 | tf_op jit(solution)/shard_map/while/body/eval_jaxpr/ppermute | solution.py:16
  338.5 23.0 %collective-permute-start = (f32[16,128,128]{2,1,0:T(8,128)}, f32[16,128,128]{2,1,0:T(8,128)S(1)}, u32[]{:S(2)}, u32[]{:S(2)}) collective-permute-start(f32[16,128,128]{2,1,0:T(8,128)} %convolution_add_fusion.6), channel_id=1, source_target_pairs={{0,1},{1,2},{2,3},{3,4},{4,5},{5,6},{6,7},{7,8},{8,9},{9,10},{10,1... | collective-permute-start | bytes 3145736 | tf_op jit(solution)/shard_map/while/body/eval_jaxpr/ppermute | solution.py:16
  364.9 22.1 %collective-permute-start = (f32[16,128,128]{2,1,0:T(8,128)}, f32[16,128,128]{2,1,0:T(8,128)S(1)}, u32[]{:S(2)}, u32[]{:S(2)}) collective-permute-start(f32[16,128,128]{2,1,0:T(8,128)} %convolution_add_fusion.6), channel_id=1, source_target_pairs={{0,1},{1,2},{2,3},{3,4},{4,5},{5,6},{6,7},{7,8},{8,9},{9,10},{10,1... | collective-permute-start | bytes 3145736 | tf_op jit(solution)/shard_map/while/body/eval_jaxpr/ppermute | solution.py:16
  390.4 22.1 %collective-permute-start = (f32[16,128,128]{2,1,0:T(8,128)}, f32[16,128,128]{2,1,0:T(8,128)S(1)}, u32[]{:S(2)}, u32[]{:S(2)}) collective-permute-start(f32[16,128,128]{2,1,0:T(8,128)} %convolution_add_fusion.6), channel_id=1, source_target_pairs={{0,1},{1,2},{2,3},{3,4},{4,5},{5,6},{6,7},{7,8},{8,9},{9,10},{10,1... | collective-permute-start | bytes 3145736 | tf_op jit(solution)/shard_map/while/body/eval_jaxpr/ppermute | solution.py:16
  415.8 22.4 %collective-permute-start = (f32[16,128,128]{2,1,0:T(8,128)}, f32[16,128,128]{2,1,0:T(8,128)S(1)}, u32[]{:S(2)}, u32[]{:S(2)}) collective-permute-start(f32[16,128,128]{2,1,0:T(8,128)} %convolution_add_fusion.6), channel_id=1, source_target_pairs={{0,1},{1,2},{2,3},{3,4},{4,5},{5,6},{6,7},{7,8},{8,9},{9,10},{10,1... | collective-permute-start | bytes 3145736 | tf_op jit(solution)/shard_map/while/body/eval_jaxpr/ppermute | solution.py:16
  441.6 21.5 %collective-permute-start = (f32[16,128,128]{2,1,0:T(8,128)}, f32[16,128,128]{2,1,0:T(8,128)S(1)}, u32[]{:S(2)}, u32[]{:S(2)}) collective-permute-start(f32[16,128,128]{2,1,0:T(8,128)} %convolution_add_fusion.6), channel_id=1, source_target_pairs={{0,1},{1,2},{2,3},{3,4},{4,5},{5,6},{6,7},{7,8},{8,9},{9,10},{10,1... | collective-permute-start | bytes 3145736 | tf_op jit(solution)/shard_map/while/body/eval_jaxpr/ppermute | solution.py:16
  466.4 20.5 %collective-permute-start = (f32[16,128,128]{2,1,0:T(8,128)}, f32[16,128,128]{2,1,0:T(8,128)S(1)}, u32[]{:S(2)}, u32[]{:S(2)}) collective-permute-start(f32[16,128,128]{2,1,0:T(8,128)} %convolution_add_fusion.6), channel_id=1, source_target_pairs={{0,1},{1,2},{2,3},{3,4},{4,5},{5,6},{6,7},{7,8},{8,9},{9,10},{10,1... | collective-permute-start | bytes 3145736 | tf_op jit(solution)/shard_map/while/body/eval_jaxpr/ppermute | solution.py:16
  490.3 19.6 %collective-permute-start = (f32[16,128,128]{2,1,0:T(8,128)}, f32[16,128,128]{2,1,0:T(8,128)S(1)}, u32[]{:S(2)}, u32[]{:S(2)}) collective-permute-start(f32[16,128,128]{2,1,0:T(8,128)} %convolution_add_fusion.6), channel_id=1, source_target_pairs={{0,1},{1,2},{2,3},{3,4},{4,5},{5,6},{6,7},{7,8},{8,9},{9,10},{10,1... | collective-permute-start | bytes 3145736 | tf_op jit(solution)/shard_map/while/body/eval_jaxpr/ppermute | solution.py:16
  513.2 18.7 %collective-permute-start = (f32[16,128,128]{2,1,0:T(8,128)}, f32[16,128,128]{2,1,0:T(8,128)S(1)}, u32[]{:S(2)}, u32[]{:S(2)}) collective-permute-start(f32[16,128,128]{2,1,0:T(8,128)} %convolution_add_fusion.6), channel_id=1, source_target_pairs={{0,1},{1,2},{2,3},{3,4},{4,5},{5,6},{6,7},{7,8},{8,9},{9,10},{10,1... | collective-permute-start | bytes 3145736 | tf_op jit(solution)/shard_map/while/body/eval_jaxpr/ppermute | solution.py:16
  535.3 18.6 %collective-permute-start = (f32[16,128,128]{2,1,0:T(8,128)}, f32[16,128,128]{2,1,0:T(8,128)S(1)}, u32[]{:S(2)}, u32[]{:S(2)}) collective-permute-start(f32[16,128,128]{2,1,0:T(8,128)} %convolution_add_fusion.6), channel_id=1, source_target_pairs={{0,1},{1,2},{2,3},{3,4},{4,5},{5,6},{6,7},{7,8},{8,9},{9,10},{10,1... | collective-permute-start | bytes 3145736 | tf_op jit(solution)/shard_map/while/body/eval_jaxpr/ppermute | solution.py:16
  557.2 19.4 %collective-permute-start = (f32[16,128,128]{2,1,0:T(8,128)}, f32[16,128,128]{2,1,0:T(8,128)S(1)}, u32[]{:S(2)}, u32[]{:S(2)}) collective-permute-start(f32[16,128,128]{2,1,0:T(8,128)} %convolution_add_fusion.6), channel_id=1, source_target_pairs={{0,1},{1,2},{2,3},{3,4},{4,5},{5,6},{6,7},{7,8},{8,9},{9,10},{10,1... | collective-permute-start | bytes 3145736 | tf_op jit(solution)/shard_map/while/body/eval_jaxpr/ppermute | solution.py:16
  579.9 20.1 %collective-permute-start = (f32[16,128,128]{2,1,0:T(8,128)}, f32[16,128,128]{2,1,0:T(8,128)S(1)}, u32[]{:S(2)}, u32[]{:S(2)}) collective-permute-start(f32[16,128,128]{2,1,0:T(8,128)} %convolution_add_fusion.6), channel_id=1, source_target_pairs={{0,1},{1,2},{2,3},{3,4},{4,5},{5,6},{6,7},{7,8},{8,9},{9,10},{10,1... | collective-permute-start | bytes 3145736 | tf_op jit(solution)/shard_map/while/body/eval_jaxpr/ppermute | solution.py:16
  603.4 20.9 %collective-permute-start = (f32[16,128,128]{2,1,0:T(8,128)}, f32[16,128,128]{2,1,0:T(8,128)S(1)}, u32[]{:S(2)}, u32[]{:S(2)}) collective-permute-start(f32[16,128,128]{2,1,0:T(8,128)} %convolution_add_fusion.6), channel_id=1, source_target_pairs={{0,1},{1,2},{2,3},{3,4},{4,5},{5,6},{6,7},{7,8},{8,9},{9,10},{10,1... | collective-permute-start | bytes 3145736 | tf_op jit(solution)/shard_map/while/body/eval_jaxpr/ppermute | solution.py:16
  636.8 13.6 collective-permute-start.1
  655.1 16.2 %collective-permute-start.1 = (bf16[16,128,128]{2,1,0:T(8,128)(2,1)}, bf16[16,128,128]{2,1,0:T(8,128)(2,1)}, u32[]{:S(2)}, u32[]{:S(2)}) collective-permute-start(bf16[16,128,128]{2,1,0:T(8,128)(2,1)} %fusion.372), channel_id=1, source_target_pairs={{1,0},{2,1},{3,2},{4,3},{5,4},{6,5},{7,6},{8,7},{9,8},{10,9},{11,1... | collective-permute-start | bytes 1572872 | tf_op jit(solution)/shard_map/while/body/eval_jaxpr/ppermute | solution.py:16
  676.0 17.3 %collective-permute-start.1 = (bf16[16,128,128]{2,1,0:T(8,128)(2,1)}, bf16[16,128,128]{2,1,0:T(8,128)(2,1)}, u32[]{:S(2)}, u32[]{:S(2)}) collective-permute-start(bf16[16,128,128]{2,1,0:T(8,128)(2,1)} %fusion.372), channel_id=1, source_target_pairs={{1,0},{2,1},{3,2},{4,3},{5,4},{6,5},{7,6},{8,7},{9,8},{10,9},{11,1... | collective-permute-start | bytes 1572872 | tf_op jit(solution)/shard_map/while/body/eval_jaxpr/ppermute | solution.py:16
  698.0 18.4 %collective-permute-start.1 = (bf16[16,128,128]{2,1,0:T(8,128)(2,1)}, bf16[16,128,128]{2,1,0:T(8,128)(2,1)}, u32[]{:S(2)}, u32[]{:S(2)}) collective-permute-start(bf16[16,128,128]{2,1,0:T(8,128)(2,1)} %fusion.372), channel_id=1, source_target_pairs={{1,0},{2,1},{3,2},{4,3},{5,4},{6,5},{7,6},{8,7},{9,8},{10,9},{11,1... | collective-permute-start | bytes 1572872 | tf_op jit(solution)/shard_map/while/body/eval_jaxpr/ppermute | solution.py:16
  721.1 19.2 %collective-permute-start.1 = (bf16[16,128,128]{2,1,0:T(8,128)(2,1)}, bf16[16,128,128]{2,1,0:T(8,128)(2,1)}, u32[]{:S(2)}, u32[]{:S(2)}) collective-permute-start(bf16[16,128,128]{2,1,0:T(8,128)(2,1)} %fusion.372), channel_id=1, source_target_pairs={{1,0},{2,1},{3,2},{4,3},{5,4},{6,5},{7,6},{8,7},{9,8},{10,9},{11,1... | collective-permute-start | bytes 1572872 | tf_op jit(solution)/shard_map/while/body/eval_jaxpr/ppermute | solution.py:16
  745.0 16.3 %collective-permute-start.1 = (bf16[16,128,128]{2,1,0:T(8,128)(2,1)}, bf16[16,128,128]{2,1,0:T(8,128)(2,1)}, u32[]{:S(2)}, u32[]{:S(2)}) collective-permute-start(bf16[16,128,128]{2,1,0:T(8,128)(2,1)} %fusion.372), channel_id=1, source_target_pairs={{1,0},{2,1},{3,2},{4,3},{5,4},{6,5},{7,6},{8,7},{9,8},{10,9},{11,1... | collective-permute-start | bytes 1572872 | tf_op jit(solution)/shard_map/while/body/eval_jaxpr/ppermute | solution.py:16
  766.0 14.5 collective-permute-start.1
  785.2 13.7 collective-permute-start.1
  803.6 12.8 collective-permute-start.1
  821.1 11.9 collective-permute-start.1
  837.7 11.4 collective-permute-start.1
  853.8 12.1 collective-permute-start.1
  870.5 12.3 collective-permute-start.1
  887.6 12.3 collective-permute-start.1
  904.6 12.3 collective-permute-start.1
  926.8 304.7 %copy-start.59 = (f32[128,8]{0,1:T(8,128)S(1)}, f32[128,8]{0,1:T(8,128)}, u32[]{:S(2)}) copy-start(f32[128,8]{0,1:T(8,128)} %copy-done.58) | copy-start | bytes 12292
  1241.4 9.0 copy-start.52
  1241.4 9.0 copy-start.54
  1241.5 9.0 copy-start.56
  1258.3 109.5 %copy-start.44 = (bf16[128,16,128]{2,0,1:T(8,128)(2,1)S(1)}, bf16[128,16,128]{2,0,1:T(8,128)(2,1)}, u32[]{:S(2)}) copy-start(bf16[128,16,128]{2,0,1:T(8,128)(2,1)} %fusion.149) | copy-start | bytes 1572868
  1259.6 109.6 %collective-permute-start.3 = (bf16[3,4096]{1,0:T(4,128)(2,1)S(1)}, bf16[3,4096]{1,0:T(4,128)(2,1)S(1)}, u32[]{:S(2)}, u32[]{:S(2)}) collective-permute-start(bf16[3,4096]{1,0:T(4,128)(2,1)S(1)} %copy.597), channel_id=1, source_target_pairs={{1,0},{2,1},{3,2},{4,3},{5,4},{6,5},{7,6},{8,7},{9,8},{10,9},{11,1... | collective-permute-start | bytes 73736 | tf_op jit(solution)/shard_map/ppermute | solution.py:16
  (91 other events, 259.7 us)
Sparse Core Ops, SparseCore 0:
  1369.3 134.1 all-reduce.20
where the time goes:
time: 1520 us; the launch traced here: 1510 us
  waiting for transfers between devices  568 us (37%)
  other arithmetic  389 us (26%)
  matrix products  225 us (15%)
  blocking collectives  106 us (7%)
  starting transfers between devices  105 us (7%)
  local copies, waits for them, and re-layouts  70.3 us (5%)
  loops' own time  34.2 us (2%)
    ppermute x32, waiting for transfers between devices, shifted(): lax.ppermute(value, axis, [(source, source + steps) for source in range(i...  438 us
    another operation x14, other arithmetic, group_head(): lax.linalg.triangular_solve(system, right_side, left_side=True, lower=Tru...  323 us
    psum x1, waiting for transfers between devices, on_device(): d_conv, d_head = lax.psum((grad_conv, grad_params), ('dp', 'ctx'))  130 us
    psum x1, blocking collectives, on_device(): d_conv, d_head = lax.psum((grad_conv, grad_params), ('dp', 'ctx'))  106 us
    ppermute x32, starting transfers between devices, shifted(): lax.ppermute(value, axis, [(source, source + steps) for source in range(i...  105 us
    dot_general x15, matrix products, backward_turn(): jnp.einsum('hvk,hkj->hvj', incoming, transposed, precision=highest)  53.1 us
    dot_general x15, matrix products, forward_turn(): jnp.einsum('hvk,hkj->hvj', incoming, transition, precision=highest)  50.3 us
    another operation x2, loops' own time, delta_core(): lax.scan(jax.checkpoint(advance), memory, (folded(queries), folded(key_ro...  33.5 us
  transfers between devices with their start and end apart: 33, of which 31 were waited for; matrix products, arithmetic and copies ran while one was open for 1% of the time, Pallas kernels for 0%

commit v1 on v0

v1 whole, which is shorter than its diff:
```python
import jax
import jax.numpy as jnp
from jax import lax
from jax.experimental import pallas as pl
from jax.experimental.pallas import tpu as pltpu
from jax.sharding import PartitionSpec as P

HEADS = 16
QK = 8
D = 128
ROWS = 128
CH = 4096
BLOCKS = 16
PACK = 3 * D + 16
HG = 4
F32 = jnp.float32
BF = jnp.bfloat16
MESH = pl.DeviceIdType.MESH
HIGHEST = lax.Precision.HIGHEST


def dot(a, b, ca=1, cb=0):
    return lax.dot_general(a, b, (((ca,), (cb,)), ((), ())), preferred_element_type=F32)


def dot_full(a, b, ca=1, cb=0):
    return lax.dot_general(
        a, b, (((ca,), (cb,)), ((), ())), preferred_element_type=F32, precision=HIGHEST
    )


def split(a):
    high = a.astype(BF)
    return high, (a - high.astype(F32)).astype(BF)


def dot3(a, b, ca=1, cb=0):
    return dot(a[0], b[0], ca, cb) + (dot(a[0], b[1], ca, cb) + dot(a[1], b[0], ca, cb))


def iota(shape, dim):
    return lax.broadcasted_iota(jnp.int32, shape, dim)


def inverses(mats):
    row, col = iota((D, D), 0), iota((D, D), 1)
    eye = (row == col).astype(F32)

    def same(bits):
        return (row >> bits) == (col >> bits)

    near = same(3)
    a8 = [jnp.where(near, a, 0.0) for a in mats]
    a8s = [split(a) for a in a8]
    a2 = [dot3(s, s) for s in a8s]
    a2s = [split(a) for a in a2]
    a3 = [dot3(s, t) for s, t in zip(a8s, a2s)]
    a4s = [split(dot3(s, s)) for s in a2s]
    ys = [eye - a + b - c for a, b, c in zip(a8, a2, a3)]
    xs = [y + dot3(split(y), s) for y, s in zip(ys, a4s)]
    for bits in range(3, 7):
        mask = same(bits + 1) & jnp.logical_not(same(bits))
        cs = [split(jnp.where(mask, a, 0.0)) for a in mats]
        xss = [split(x) for x in xs]
        xc = [split(dot3(x, c)) for x, c in zip(xss, cs)]
        xs = [x - dot3(t, s) for x, t, s in zip(xs, xc, xss)]
    return xs


def kernel(
    x_ref, w_ref, gate_ref, hp_ref, len_ref, dcore_ref,
    core_ref, dmix_ref, dgate_ref, red_ref,
    xs, ys, qs, ks, links, lks, gt, gts, d_s, dkk_s, p_s, x_s, uv_s, wq_s, w2_s, r0_s, ol_s,
    snd, rcv, s_snd, g_snd, s_rcv, g_rcv, h_snd, h_rcv, e_snd, e_rcv, dgt,
    snd_sem, rcv_sem, s_ssem, s_rsem, g_ssem, g_rsem, h_sem, e_sem,
):
    me = lax.axis_index("ctx")
    first_pos = me * ROWS

    barrier = pltpu.get_barrier_semaphore()

    def greet(i, _):
        pl.semaphore_signal(
            barrier, inc=1, device_id={"ctx": lax.rem(me + i, BLOCKS)}, device_id_type=MESH
        )
        return 0

    lax.fori_loop(1, BLOCKS, greet, 0)

    xs[pl.ds(8, ROWS), :] = x_ref[...].astype(F32)
    tail = [
        xs[pl.ds(133 + r, 1), pl.ds(1024 * p, 1024)] for r in range(3) for p in range(4)
    ] + [jnp.zeros((4, 1024), F32)]
    h_snd[...] = jnp.concatenate(tail, axis=0).astype(BF)

    pl.semaphore_wait(barrier, BLOCKS - 1)

    def halo_copy():
        return pltpu.make_async_remote_copy(
            src_ref=h_snd, dst_ref=h_rcv, send_sem=h_sem.at[0], recv_sem=h_sem.at[1],
            device_id={"ctx": lax.rem(me + 1, BLOCKS)}, device_id_type=MESH,
        )

    halo_copy().start()

    row, col = iota((ROWS, D), 0), iota((ROWS, D), 1)
    low = row >= col
    strict = row > col
    ends = []
    total = 0
    for i in range(8):
        total = total + len_ref[0, i]
        ends.append(total)

    def doc_of(pos):
        found = jnp.zeros(pos.shape, jnp.int32)
        for e in ends:
            found = found + jnp.where(e <= pos, 1, 0)
        return found

    doc_col = doc_of(first_pos + row)
    doc_row = doc_of(first_pos + col)
    lks[...] = jnp.where((doc_col == doc_row) & low, 1.0, 0.0)
    for j in range(3):
        links[j] = jnp.where(doc_of(first_pos + row - 3 + j) == doc_col, 1.0, 0.0)
    doc_row16 = doc_row[:HEADS]
    doc_before = doc_of(jnp.full((HEADS, D), first_pos - 1, jnp.int32))
    doc_last = doc_of(jnp.full((HEADS, D), first_pos + ROWS - 1, jnp.int32))

    eye32 = (iota((32, 32), 0) == iota((32, 32), 1)).astype(F32)
    eye16 = (iota((16, 16), 0) == iota((16, 16), 1)).astype(F32)
    gates = dot_full(eye32, gate_ref[...], 1, 1)
    params = dot_full(eye16, hp_ref[...], 1, 1)
    scale = -jnp.exp(params[:, 0:1])
    z = gates[:HEADS] + params[:, 1:2]
    decay = scale * (jnp.maximum(z, 0.0) + jnp.log1p(jnp.exp(-jnp.abs(z))))
    ez = scale / (1.0 + jnp.exp(-z))
    beta = 1.0 / (1.0 + jnp.exp(-gates[HEADS:]))
    upto = jnp.where(row <= col, 1.0, 0.0)
    summed = dot_full(decay, upto)
    carried = jnp.exp(summed) * (doc_row16 == doc_before).astype(F32)
    to_end = jnp.exp(jnp.minimum(summed[:, D - 1 : D] - summed, 0.0)) * (
        doc_row16 == doc_last
    ).astype(F32)
    gts[0] = decay
    gts[1] = ez
    gts[2] = beta
    rows8 = jnp.stack(
        [summed, beta, carried, to_end, beta * carried, summed, summed, summed], axis=1
    )
    gt[...] = rows8

    halo_copy().wait()
    inside = jnp.where(me > 0, 1.0, 0.0)
    hv = h_rcv[...].astype(F32) * inside
    for r in range(3):
        for p in range(4):
            xs[pl.ds(5 + r, 1), pl.ds(1024 * p, 1024)] = hv[4 * r + p : 4 * r + p + 1]

    def lanes(block):
        return pl.ds(pl.multiple_of(block * D, D), D)

    def taps(j, block):
        t = xs[pl.ds(5 + j, ROWS), lanes(block)]
        return t if j == 3 else t * links[j]

    def conv(block):
        y = taps(3, block) * w_ref[3:4, lanes(block)]
        for j in range(3):
            y = y + taps(j, block) * w_ref[j : j + 1, lanes(block)]
        ys[:, lanes(block)] = y
        return y / (1.0 + jnp.exp(-y))

    def columns(h):
        t = jnp.transpose(gt[h])
        return [t[:, i : i + 1] for i in range(5)]

    def a_last(h):
        return gt[h][2:3, D - 1 : D]

    def pack_copy(h, source):
        return pltpu.make_async_remote_copy(
            src_ref=snd.at[h], dst_ref=rcv.at[source], send_sem=snd_sem.at[h],
            recv_sem=rcv_sem.at[source], device_id={"ctx": h}, device_id_type=MESH,
        )

    def forward(step, _):
        group = lax.rem(step + me, HEADS // HG)
        nq = HG // 2
        qk = [group * nq + i for i in range(nq)]
        heads = [group * HG + i for i in range(HG)]
        kk, qq, kf, qf = [], [], [], []
        for j in qk:
            m = conv(j)
            q = m * (lax.rsqrt(jnp.sum(m * m, axis=1, keepdims=True) + 1e-6) * D**-0.5)
            m = conv(QK + j)
            k = m * lax.rsqrt(jnp.sum(m * m, axis=1, keepdims=True) + 1e-6)
            qs[j] = q
            ks[j] = k
            k2, q2 = split(k), split(q)
            kk.append(dot3(k2, k2, 1, 1))
            qq.append(dot3(q2, k2, 1, 1))
            kf.append(k)
            qf.append(q)
        vs = [conv(2 * QK + h) for h in heads]
        cols = [columns(h) for h in heads]
        lk = lks[...]
        mats, ps = [], []
        for i, h in enumerate(heads):
            spans = lk * jnp.exp(jnp.minimum(cols[i][0] - gt[h][0:1], 0.0))
            dkk = jnp.where(strict, spans * kk[i // 2], 0.0)
            p = spans * qq[i // 2]
            d_s[h] = spans
            dkk_s[h] = dkk
            p_s[h] = p
            ps.append(p.astype(BF))
            mats.append(cols[i][1] * dkk)
        xinv = inverses(mats)
        for i, h in enumerate(heads):
            x_s[h] = xinv[i]
            right = jnp.concatenate([cols[i][1] * vs[i], cols[i][4] * kf[i // 2]], axis=1)
            uvw = dot3(split(xinv[i]), split(right))
            uvwb = uvw.astype(BF)
            uv_s[h] = uvw[:, :D]
            wq_s[h, 0:ROWS] = uvwb[:, D:]
            pw = dot(ps[i], uvwb)
            ol_s[h] = pw[:, :D]
            qc = (cols[i][2] * qf[i // 2] - pw[:, D:]).astype(BF)
            wq_s[h, ROWS : 2 * ROWS] = qc
            dk = (cols[i][3] * kf[i // 2]).astype(BF)
            nb = dot(uvwb, dk, 0, 0)
            gl = dot(dcore_ref[:, lanes(h)], qc, 0, 0)
            snd[h, 0:D] = nb[D:].astype(BF)
            snd[h, D : 2 * D] = nb[:D].astype(BF)
            snd[h, 2 * D : 3 * D] = gl.astype(BF)
            al = jnp.broadcast_to(a_last(h), (16, D))
            t0 = al.astype(BF).astype(F32)
            t1 = (al - t0).astype(BF).astype(F32)
            t2 = al - t0 - t1
            r16 = iota((16, D), 0)
            snd[h, 3 * D : PACK] = jnp.where(
                r16 == 0, t0, jnp.where(r16 == 1, t1, jnp.where(r16 == 2, t2, 0.0))
            ).astype(BF)
        for h in heads:
            @pl.when(h != me)
            def _():
                pack_copy(h, me).start()
        return 0

    lax.fori_loop(0, HEADS // HG, forward, 0)
    rcv[me] = snd[me]

    def aside(step, _):
        heads = [step * HG + i for i in range(HG)]
        for i, h in enumerate(heads):
            cols = columns(h)
            zz = dot(p_s[h].astype(BF), dcore_ref[:, lanes(h)], 0, 0)
            dk = cols[3] * ks[h // 2]
            out = dot3(split(x_s[h]), split(jnp.concatenate([zz, dk], axis=1)), 0, 0)
            r0_s[h] = out[:, :D]
            w2_s[h] = out[:, D:].astype(BF)
        return 0

    lax.fori_loop(0, HEADS // HG, aside, 0)

    def wait_pack(i, _):
        pack_copy(lax.rem(me + i, BLOCKS), lax.rem(me + i, BLOCKS)).wait_recv()
        return 0

    lax.fori_loop(1, BLOCKS, wait_pack, 0)

    def s_copy(block, head):
        return pltpu.make_async_remote_copy(
            src_ref=s_snd.at[block], dst_ref=s_rcv.at[head], send_sem=s_ssem.at[block],
            recv_sem=s_rsem.at[head], device_id={"ctx": block}, device_id_type=MESH,
        )

    def g_copy(block, head):
        return pltpu.make_async_remote_copy(
            src_ref=g_snd.at[block], dst_ref=g_rcv.at[head], send_sem=g_ssem.at[block],
            recv_sem=g_rsem.at[head], device_id={"ctx": block}, device_id_type=MESH,
        )

    def send_state(block, state):
        s_snd[block] = state

        @pl.when(block != me)
        def _():
            s_copy(block, me).start()

    def send_grad(block, grad):
        g_snd[block] = grad

        @pl.when(block != me)
        def _():
            g_copy(block, me).start()

    zero = jnp.zeros((D, D), F32)
    send_state(0, zero.astype(BF))
    send_grad(BLOCKS - 1, zero.astype(BF))

    def scalar_of(block):
        t = rcv[block, 3 * D : PACK].astype(F32)
        return t[0:1] + t[1:2] + t[2:3]

    def turn(i, carry):
        state, grad = carry
        b = BLOCKS - 1 - i
        state = (
            scalar_of(i) * state
            - dot(state.astype(BF), rcv[i, 0:D])
            + rcv[i, D : 2 * D].astype(F32)
        )
        grad = (
            scalar_of(b) * grad
            - dot(grad.astype(BF), rcv[b, 0:D], 1, 1)
            + rcv[b, 2 * D : 3 * D].astype(F32)
        )
        send_state(i + 1, state.astype(BF))
        send_grad(b - 1, grad.astype(BF))
        return state, grad

    lax.fori_loop(0, BLOCKS - 1, turn, (zero, zero))
    s_rcv[me] = s_snd[me]
    g_rcv[me] = g_snd[me]

    lane = col
    row8 = row[:8]

    def conv_back(block, dm):
        y = ys[:, lanes(block)]
        sig = 1.0 / (1.0 + jnp.exp(-y))
        dy = dm * (sig * (1.0 + y * (1.0 - sig)))
        red_ref[3:4, lanes(block)] = jnp.sum(dy * taps(3, block), axis=0, keepdims=True)
        own = dy * w_ref[3:4, lanes(block)]
        spill = jnp.zeros((8, D), F32)
        for j in range(3):
            ej = dy * links[j]
            red_ref[j : j + 1, lanes(block)] = jnp.sum(
                ej * xs[pl.ds(5 + j, ROWS), lanes(block)], axis=0, keepdims=True
            )
            turned = pltpu.roll(ej * w_ref[j : j + 1, lanes(block)], ROWS - 3 + j, 0)
            wrapped = row >= ROWS - 3 + j
            own = own + jnp.where(wrapped, 0.0, turned)
            spill = spill + jnp.where(row8 >= 5 + j, turned[ROWS - 8 :], 0.0)
        dmix_ref[:, lanes(block)] = own.astype(BF)
        e_snd[0:8, lanes(block)] = own[ROWS - 8 :]
        e_snd[8:16, lanes(block)] = spill

    def backward(step, _):
        group = lax.rem(step + me, HEADS // HG)
        nq = HG // 2
        qk = [group * nq + i for i in range(nq)]
        heads = [group * HG + i for i in range(HG)]
        for h in heads:
            @pl.when(h != me)
            def _():
                s_copy(h, h).wait_recv()
                g_copy(h, h).wait_recv()
        packed = jnp.zeros((ROWS, D), F32)
        colsums, lasts = [], []
        for n, j in enumerate(qk):
            k, q = ks[j], qs[j]
            bs = es = dq = dk = None
            for i in (2 * n, 2 * n + 1):
                h = heads[i]
                _, bet, car, end, bcar = columns(h)
                s, g = s_rcv[h], g_rcv[h]
                do = dcore_ref[:, lanes(h)]
                t = dot(wq_s[h], s, 1, 1)
                u = (uv_s[h] - t[:ROWS]).astype(BF)
                core_ref[:, lanes(h)] = (ol_s[h] + t[ROWS:]).astype(BF)
                r = r0_s[h] + dot(w2_s[h], g, 1, 1)
                dr = jnp.concatenate([do, r.astype(BF)], axis=0)
                t2 = dot(dr, s)
                dos, rs = t2[:ROWS], t2[ROWS:]
                t3 = dot(dr, u, 1, 1)
                dp, da = t3[:ROWS], -t3[ROWS:]
                ug = dot(u, g)
                spans = d_s[h]
                t1 = da * dkk_s[h]
                f = dp * p_s[h] + bet * t1
                yv = ys[:, lanes(2 * QK + h)]
                v = yv / (1.0 + jnp.exp(-yv))
                krs = car * k * rs
                dkug = end * k * ug
                dbeta = jnp.sum(r * v - krs + t1, axis=1, keepdims=True)
                dc = jnp.sum(f + car * q * dos - bet * krs - dkug, axis=1, keepdims=True)
                packed = packed + jnp.where(lane == 2 * i, dc, 0.0)
                packed = packed + jnp.where(lane == 2 * i + 1, dbeta, 0.0)
                colsums.append(jnp.sum(f, axis=0, keepdims=True))
                lasts.append(
                    jnp.sum(
                        jnp.sum(dkug, axis=0, keepdims=True)
                        + a_last(h)
                        * jnp.sum(g.astype(F32) * s.astype(F32), axis=0, keepdims=True),
                        axis=1, keepdims=True,
                    )
                )
                bq = dp * spans
                e = jnp.where(strict, bet * da * spans, 0.0)
                dqi = car * dos
                dki = end * ug - bcar * rs
                bs = bq if bs is None else bs + bq
                es = e if es is None else es + e
                dq = dqi if dq is None else dq + dqi
                dk = dki if dk is None else dk + dki
                conv_back(2 * QK + h, bet * r)
            be = jnp.concatenate([bs, es], axis=0).astype(BF)
            kb = k.astype(BF)
            t4 = dot(be, kb)
            t5 = dot(be, jnp.concatenate([q.astype(BF), kb], axis=0), 0, 0)
            dq = dq + t4[:ROWS]
            dk = dk + t4[ROWS:] + t5
            y = ys[:, lanes(j)]
            m = y / (1.0 + jnp.exp(-y))
            rq = lax.rsqrt(jnp.sum(m * m, axis=1, keepdims=True) + 1e-6)
            dm = rq * (D**-0.5) * (dq - m * (rq * rq * jnp.sum(m * dq, axis=1, keepdims=True)))
            conv_back(j, dm)
            y = ys[:, lanes(QK + j)]
            m = y / (1.0 + jnp.exp(-y))
            rk = lax.rsqrt(jnp.sum(m * m, axis=1, keepdims=True) + 1e-6)
            dm = rk * (dk - m * (rk * rk * jnp.sum(m * dk, axis=1, keepdims=True)))
            conv_back(QK + j, dm)
        rows = jnp.transpose(packed)
        lane1 = lane[:1]
        for i, h in enumerate(heads):
            dgt[0, pl.ds(h, 1), :] = (
                rows[2 * i : 2 * i + 1] - colsums[i] + jnp.where(lane1 == D - 1, lasts[i], 0.0)
            )
            dgt[1, pl.ds(h, 1), :] = rows[2 * i + 1 : 2 * i + 2]
        return 0

    lax.fori_loop(0, HEADS // HG, backward, 0)

    spill = e_snd[8:16, :]
    h_snd[...] = jnp.concatenate(
        [spill[5 + r : 6 + r, 1024 * p : 1024 * p + 1024] for r in range(3) for p in range(4)]
        + [jnp.zeros((4, 1024), F32)],
        axis=0,
    ).astype(BF)
    back = pltpu.make_async_remote_copy(
        src_ref=h_snd, dst_ref=e_rcv, send_sem=e_sem.at[0], recv_sem=e_sem.at[1],
        device_id={"ctx": lax.rem(me + BLOCKS - 1, BLOCKS)}, device_id_type=MESH,
    )
    back.start()

    dg = dot_full(dgt[0], jnp.where(row >= col, 1.0, 0.0))
    dz = dg * gts[1]
    bet = gts[2]
    both = jnp.concatenate([dz, dgt[1] * bet * (1.0 - bet)], axis=0)
    dgate_ref[...] = dot_full(jnp.where(row == col, 1.0, 0.0), both, 1, 1)
    ones = jnp.ones((1, D), F32)
    red_ref[4:8, :] = jnp.zeros((4, CH), F32)
    red_ref[4:5, 0:HEADS] = dot_full(ones, dg * gts[0], 1, 1)
    red_ref[5:6, 0:HEADS] = dot_full(ones, dz, 1, 1)

    back.wait()
    before_last = jnp.where(me < BLOCKS - 1, 1.0, 0.0)
    ev = e_rcv[...].astype(F32) * before_last
    for p in range(4):
        pieces = [jnp.zeros((5, 1024), F32)] + [ev[4 * r + p : 4 * r + p + 1] for r in range(3)]
        part = e_snd[0:8, 1024 * p : 1024 * p + 1024] + jnp.concatenate(pieces, axis=0)
        old = dmix_ref[ROWS - 16 :, 1024 * p : 1024 * p + 1024].astype(F32)
        dmix_ref[ROWS - 16 :, 1024 * p : 1024 * p + 1024] = jnp.concatenate(
            [old[:8], part], axis=0
        ).astype(BF)

    def drain(i, _):
        other = lax.rem(me + i, BLOCKS)
        pack_copy(other, me).wait_send()
        s_copy(other, me).wait_send()
        g_copy(other, me).wait_send()
        return 0

    lax.fori_loop(1, BLOCKS, drain, 0)


def on_device(mixed_in, conv_weight, gate_in, head_params, doc_lengths, d_core):
    vmem = pl.BlockSpec(memory_space=pltpu.VMEM)
    mat = (HEADS, D, D)
    scratch = [
        pltpu.VMEM((ROWS + 8, CH), F32),
        pltpu.VMEM((ROWS, CH), F32),
        pltpu.VMEM((QK, D, D), F32),
        pltpu.VMEM((QK, D, D), F32),
        pltpu.VMEM((3, ROWS, D), F32),
        pltpu.VMEM((ROWS, D), F32),
        pltpu.VMEM((HEADS, 8, D), F32),
        pltpu.VMEM((3, HEADS, D), F32),
        pltpu.VMEM(mat, F32),
        pltpu.VMEM(mat, F32),
        pltpu.VMEM(mat, F32),
        pltpu.VMEM(mat, F32),
        pltpu.VMEM(mat, F32),
        pltpu.VMEM((HEADS, 2 * D, D), BF),
        pltpu.VMEM(mat, BF),
        pltpu.VMEM(mat, F32),
        pltpu.VMEM(mat, F32),
        pltpu.VMEM((HEADS, PACK, D), BF),
        pltpu.VMEM((HEADS, PACK, D), BF),
        pltpu.VMEM(mat, BF),
        pltpu.VMEM(mat, BF),
        pltpu.VMEM(mat, BF),
        pltpu.VMEM(mat, BF),
        pltpu.VMEM((16, 1024), BF),
        pltpu.VMEM((16, 1024), BF),
        pltpu.VMEM((16, CH), F32),
        pltpu.VMEM((16, 1024), BF),
        pltpu.VMEM((2, HEADS, D), F32),
        pltpu.SemaphoreType.DMA((BLOCKS,)),
        pltpu.SemaphoreType.DMA((BLOCKS,)),
        pltpu.SemaphoreType.DMA((BLOCKS,)),
        pltpu.SemaphoreType.DMA((BLOCKS,)),
        pltpu.SemaphoreType.DMA((BLOCKS,)),
        pltpu.SemaphoreType.DMA((BLOCKS,)),
        pltpu.SemaphoreType.DMA((2,)),
        pltpu.SemaphoreType.DMA((2,)),
    ]
    core, dmix, dgate, red = pl.pallas_call(
        kernel,
        out_shape=(
            jax.ShapeDtypeStruct((ROWS, HEADS * D), BF),
            jax.ShapeDtypeStruct((ROWS, CH), BF),
            jax.ShapeDtypeStruct((ROWS, 2 * HEADS), F32),
            jax.ShapeDtypeStruct((8, CH), F32),
        ),
        in_specs=[vmem, vmem, vmem, vmem, pl.BlockSpec(memory_space=pltpu.SMEM), vmem],
        out_specs=(vmem, vmem, vmem, vmem),
        scratch_shapes=scratch,
        compiler_params=pltpu.CompilerParams(
            collective_id=0, has_side_effects=True, vmem_limit_bytes=56 * 1024 * 1024
        ),
        name="delta_mix",
    )(mixed_in[0], conv_weight, gate_in[0], head_params, doc_lengths, d_core[0])
    red = lax.psum(red, ("dp", "ctx"))
    return core[None], dmix[None], dgate[None], red[:4], red[4:6, :HEADS]


def solution(mesh):
    return jax.shard_map(
        on_device,
        mesh=mesh,
        in_specs=(
            P("dp", "ctx", None),
            P(),
            P("dp", "ctx", None),
            P(),
            P("dp", None),
            P("dp", "ctx", None),
        ),
        out_specs=(P("dp", "ctx", None), P("dp", "ctx", None), P("dp", "ctx", None), P(), P()),
        check_vma=False,
    )
```

time: 1520 us -> 242 us (0.16)
  waiting for transfers between devices: 568 us -> 142 us
  other arithmetic: 389 us -> 0 us
  matrix products: 225 us -> 0 us
  blocking collectives: 106 us -> 0 us
  starting transfers between devices: 105 us -> 0.04 us
  Pallas kernels: 0 us -> 76.8 us
  local copies, waits for them, and re-layouts: 70.3 us -> 8.68 us
  loops' own time: 34.2 us -> 0 us
    ppermute x32 -> x0, waiting for transfers between devices: 438 us -> none  [shifted(): lax.ppermute(value, axis, [(source, source + steps) for source in range(i...]
    another operation x23 -> x0, other arithmetic: 330 us -> none  [the longest x14 323 us: group_head(): lax.linalg.triangular_solve(system, right_side, left_side=True, lower=Tru...]
    dot_general x80 -> x0, matrix products: 211 us -> none  [the longest x15 53.1 us: backward_turn(): jnp.einsum('hvk,hkj->hvj', incoming, transposed, precision=highest)]
    psum x1 -> x0, blocking collectives: 106 us -> none  [on_device(): d_conv, d_head = lax.psum((grad_conv, grad_params), ('dp', 'ctx'))]
    ppermute x32 -> x0, starting transfers between devices: 105 us -> none  [shifted(): lax.ppermute(value, axis, [(source, source + steps) for source in range(i...]
    pallas_call x0 -> x1, Pallas kernels: none -> 76.8 us  [on_device(): pl.pallas_call(kernel, out_shape=(jax.ShapeDtypeStruct((ROWS, HEADS * D),...]
    another operation x4 -> x0, loops' own time: 34.2 us -> none  [the longest x2 33.5 us: delta_core(): lax.scan(jax.checkpoint(advance), memory, (folded(queries), folded(key_ro...]
    convert_element_type x22 -> x0, other arithmetic: 20.4 us -> none  [the longest x15 17 us: backward_turn(): shifted(leaving.astype(jnp.bfloat16), 'ctx', -1).astype(leaving.dtype)]
  transfers between devices with their start and end apart: 33 -> 1, of which waited for: 31 -> 1; matrix products, arithmetic and copies ran while one was open for 1% -> 1% of each run, Pallas kernels for 0% -> 0%
where the time goes in v1:
time: 242 us
  waiting for transfers between devices  142 us (59%)
  Pallas kernels  76.8 us (32%)
  between operations  14 us (6%)
  local copies, waits for them, and re-layouts  8.68 us (4%)
    psum x1, waiting for transfers between devices, on_device(): red = lax.psum(red, ('dp', 'ctx'))  142 us
    pallas_call x1, Pallas kernels, on_device(): pl.pallas_call(kernel, out_shape=(jax.ShapeDtypeStruct((ROWS, HEADS * D),...  76.8 us
    unnamed x6, local copies, waits for them, and re-layouts  5.9 us
  transfers between devices with their start and end apart: 1, of which 1 were waited for; matrix products, arithmetic and copies ran while one was open for 1% of the time, Pallas kernels for 0%

profile of v1, /device:TPU:1, one launch (start us, length us, event | category | flops | bytes accessed | tf_op | source)
XLA Modules:
  0.0 241.8 jit_solution(304469543096474173)
XLA Ops:
  7.2 0.0 all-reduce.2.cloned.1.call-start
  7.2 1.4 copy.11
  8.7 76.8 %delta_mix.1 = (bf16[128,2048]{1,0:T(8,128)(2,1)}, bf16[128,4096]{1,0:T(8,128)(2,1)}, f32[128,32]{1,0:T(8,128)}, f32[8,4096]{1,0:T(8,128)}) custom-call(bf16[128,4096]{1,0:T(8,128)(2,1)} %bitcast.6, f32[4,4096]{1,0:T(4,128)} %w_ref.1, f32[128,32]{1,0:T(8,128)} %bitcast.10, f32[2,16]{1,0:T(2,128)} %hp_ref.1, s32[1,8]{1,0:T(1,128)} %len_ref.1, ...), custom_call_target="tpu_custom_call" | custom-call | tf_op jit(solution)/shard_map/delta_mix/pallas_call | solution.py:520
  85.4 0.0 copy-start
  85.4 0.0 all-reduce.2.cloned.1.call-update
  85.5 1.6 copy.12
  87.1 142.3 %all-reduce.2.cloned.1.call-done = f32[8,4096]{1,0:T(8,128)} async-done(((f32[8,4096]{1,0:T(8,128)}), f32[8,4096]{1,0:T(8,128)}) %all-reduce.2.cloned.1.call-update) | async-done | bytes 131088 | tf_op jit(solution)/shard_map/psum | solution.py:536
  229.3 1.5 slice.8
  230.9 1.2 slice.9
  232.1 1.9 copy.16
  234.0 0.0 copy-done
  234.0 1.0 copy.17
Async XLA Ops:
  7.2 222.2 %all-reduce.2.cloned.1.call-start = ((), (), s32[]{:S(2)}) async-start(), calls=%async_computation | async-start | bytes 262144 | tf_op jit(solution)/shard_map/psum | solution.py:536
  85.4 148.6 %copy-start = (bf16[128,4096]{1,0:T(8,128)(2,1)S(1)}, bf16[128,4096]{1,0:T(8,128)(2,1)}, u32[]{:S(2)}) copy-start(bf16[128,4096]{1,0:T(8,128)(2,1)} %get-tuple-element.10) | copy-start | bytes 3145732
Sparse Core Ops, SparseCore 0:
  85.6 143.7 all-reduce.1

commit v2 on v1

--- a/solution.py
+++ b/solution.py
@@ -12,7 +12,11 @@
 CH = 4096
 BLOCKS = 16
 PACK = 3 * D + 16
+FG = 8
 HG = 4
+ASIDE = 2
+DP = 8
+PIECE = CH // BLOCKS
 F32 = jnp.float32
 BF = jnp.bfloat16
 MESH = pl.DeviceIdType.MESH
@@ -35,7 +39,11 @@
 
 
 def dot3(a, b, ca=1, cb=0):
-    return dot(a[0], b[0], ca, cb) + (dot(a[0], b[1], ca, cb) + dot(a[1], b[0], ca, cb))
+    left = jnp.concatenate(a, axis=ca)
+    wide = jnp.concatenate(b, axis=1 - cb)
+    n = b[0].shape[1 - cb]
+    t = dot(left, jnp.concatenate([wide, wide], axis=cb), ca, cb)
+    return t[:, :n] + t[:, n:]
 
 
 def iota(shape, dim):
@@ -69,12 +77,14 @@
 
 def kernel(
     x_ref, w_ref, gate_ref, hp_ref, len_ref, dcore_ref,
-    core_ref, dmix_ref, dgate_ref, red_ref,
+    core_ref, dmix_ref, dgate_ref, dconv_ref, dhead_ref,
     xs, ys, qs, ks, links, lks, gt, gts, d_s, dkk_s, p_s, x_s, uv_s, wq_s, w2_s, r0_s, ol_s,
-    snd, rcv, s_snd, g_snd, s_rcv, g_rcv, h_snd, h_rcv, e_snd, e_rcv, dgt,
+    snd, rcv, s_snd, g_snd, s_rcv, g_rcv, h_snd, h_rcv, e_snd, e_rcv, dgo, u_s, dos_s, dp_s, red, r1, r2, r3,
     snd_sem, rcv_sem, s_ssem, s_rsem, g_ssem, g_rsem, h_sem, e_sem,
+    r1_ssem, r1_rsem, r2_ssem, r2_rsem, r3_ssem, r3_rsem,
 ):
     me = lax.axis_index("ctx")
+    mine = lax.axis_index("dp")
     first_pos = me * ROWS
 
     barrier = pltpu.get_barrier_semaphore()
@@ -86,6 +96,14 @@
         return 0
 
     lax.fori_loop(1, BLOCKS, greet, 0)
+
+    def greet_dp(i, _):
+        pl.semaphore_signal(
+            barrier, inc=1, device_id={"dp": lax.rem(mine + i, DP)}, device_id_type=MESH
+        )
+        return 0
+
+    lax.fori_loop(1, DP, greet_dp, 0)
 
     xs[pl.ds(8, ROWS), :] = x_ref[...].astype(F32)
     tail = [
@@ -93,7 +111,7 @@
     ] + [jnp.zeros((4, 1024), F32)]
     h_snd[...] = jnp.concatenate(tail, axis=0).astype(BF)
 
-    pl.semaphore_wait(barrier, BLOCKS - 1)
+    pl.semaphore_wait(barrier, BLOCKS + DP - 2)
 
     def halo_copy():
         return pltpu.make_async_remote_copy(
@@ -127,9 +145,8 @@
     doc_before = doc_of(jnp.full((HEADS, D), first_pos - 1, jnp.int32))
     doc_last = doc_of(jnp.full((HEADS, D), first_pos + ROWS - 1, jnp.int32))
 
-    eye32 = (iota((32, 32), 0) == iota((32, 32), 1)).astype(F32)
     eye16 = (iota((16, 16), 0) == iota((16, 16), 1)).astype(F32)
-    gates = dot_full(eye32, gate_ref[...], 1, 1)
+    gates = gate_ref[...]
     params = dot_full(eye16, hp_ref[...], 1, 1)
     scale = -jnp.exp(params[:, 0:1])
     z = gates[:HEADS] + params[:, 1:2]
@@ -142,9 +159,11 @@
     to_end = jnp.exp(jnp.minimum(summed[:, D - 1 : D] - summed, 0.0)) * (
         doc_row16 == doc_last
     ).astype(F32)
-    gts[0] = decay
-    gts[1] = ez
-    gts[2] = beta
+    for n in range(HEADS // HG):
+        part = slice(n * HG, n * HG + HG)
+        gts[0, n] = decay[part]
+        gts[1, n] = ez[part]
+        gts[2, n] = beta[part]
     rows8 = jnp.stack(
         [summed, beta, carried, to_end, beta * carried, summed, summed, summed], axis=1
     )
@@ -185,10 +204,10 @@
         )
 
     def forward(step, _):
-        group = lax.rem(step + me, HEADS // HG)
-        nq = HG // 2
+        group = lax.rem(step + me, HEADS // FG)
+        nq = FG // 2
         qk = [group * nq + i for i in range(nq)]
-        heads = [group * HG + i for i in range(HG)]
+        heads = [group * FG + i for i in range(FG)]
         kk, qq, kf, qf = [], [], [], []
         for j in qk:
             m = conv(j)
@@ -247,7 +266,7 @@
                 pack_copy(h, me).start()
         return 0
 
-    lax.fori_loop(0, HEADS // HG, forward, 0)
+    lax.fori_loop(0, HEADS // FG, forward, 0)
     rcv[me] = snd[me]
 
     def aside(step, _):
@@ -261,7 +280,7 @@
             w2_s[h] = out[:, D:].astype(BF)
         return 0
 
-    lax.fori_loop(0, HEADS // HG, aside, 0)
+    lax.fori_loop(0, ASIDE, aside, 0)
 
     def wait_pack(i, _):
         pack_copy(lax.rem(me + i, BLOCKS), lax.rem(me + i, BLOCKS)).wait_recv()
@@ -288,16 +307,9 @@
         def _():
             s_copy(block, me).start()
 
-    def send_grad(block, grad):
-        g_snd[block] = grad
-
-        @pl.when(block != me)
-        def _():
-            g_copy(block, me).start()
-
     zero = jnp.zeros((D, D), F32)
     send_state(0, zero.astype(BF))
-    send_grad(BLOCKS - 1, zero.astype(BF))
+    g_snd[BLOCKS - 1] = zero.astype(BF)
 
     def scalar_of(block):
         t = rcv[block, 3 * D : PACK].astype(F32)
@@ -317,26 +329,35 @@
             + rcv[b, 2 * D : 3 * D].astype(F32)
         )
         send_state(i + 1, state.astype(BF))
-        send_grad(b - 1, grad.astype(BF))
+        g_snd[b - 1] = grad.astype(BF)
         return state, grad
 
     lax.fori_loop(0, BLOCKS - 1, turn, (zero, zero))
+
+    def send_grad(i, _):
+        other = lax.rem(me + i, BLOCKS)
+        g_copy(other, me).start()
+        return 0
+
+    lax.fori_loop(1, BLOCKS, send_grad, 0)
     s_rcv[me] = s_snd[me]
     g_rcv[me] = g_snd[me]
+    lax.fori_loop(ASIDE, HEADS // HG, aside, 0)
 
     lane = col
     row8 = row[:8]
 
-    def conv_back(block, dm):
+    def conv_back(block, piece, half, dm):
+        at = pl.ds(half * D, D)
         y = ys[:, lanes(block)]
         sig = 1.0 / (1.0 + jnp.exp(-y))
         dy = dm * (sig * (1.0 + y * (1.0 - sig)))
-        red_ref[3:4, lanes(block)] = jnp.sum(dy * taps(3, block), axis=0, keepdims=True)
+        red[piece, 3:4, at] = jnp.sum(dy * taps(3, block), axis=0, keepdims=True)
         own = dy * w_ref[3:4, lanes(block)]
         spill = jnp.zeros((8, D), F32)
         for j in range(3):
             ej = dy * links[j]
-            red_ref[j : j + 1, lanes(block)] = jnp.sum(
+            red[piece, j : j + 1, at] = jnp.sum(
                 ej * xs[pl.ds(5 + j, ROWS), lanes(block)], axis=0, keepdims=True
             )
             turned = pltpu.roll(ej * w_ref[j : j + 1, lanes(block)], ROWS - 3 + j, 0)
@@ -347,15 +368,48 @@
         e_snd[0:8, lanes(block)] = own[ROWS - 8 :]
         e_snd[8:16, lanes(block)] = spill
 
-    def backward(step, _):
+    def group_of(step):
         group = lax.rem(step + me, HEADS // HG)
-        nq = HG // 2
-        qk = [group * nq + i for i in range(nq)]
-        heads = [group * HG + i for i in range(HG)]
+        return group, [group * HG + i for i in range(HG)]
+
+    def from_state(step, _):
+        _, heads = group_of(step)
         for h in heads:
             @pl.when(h != me)
             def _():
                 s_copy(h, h).wait_recv()
+        for h in heads:
+            s = s_rcv[h]
+            do = dcore_ref[:, lanes(h)]
+            t = dot(wq_s[h], s, 1, 1)
+            u = (uv_s[h] - t[:ROWS]).astype(BF)
+            core_ref[:, lanes(h)] = (ol_s[h] + t[ROWS:]).astype(BF)
+            u_s[h] = u
+            dos_s[h] = dot(do, s)
+            dp_s[h] = dot(do, u, 1, 1)
+        return 0
+
+    lax.fori_loop(0, HEADS // HG, from_state, 0)
+
+    suffix = jnp.where(row >= col, 1.0, 0.0)
+    red[:, 4:8, :] = jnp.zeros((BLOCKS, 4, PIECE), F32)
+
+    def red_copy(piece, source):
+        return pltpu.make_async_remote_copy(
+            src_ref=red.at[piece], dst_ref=r1.at[source], send_sem=r1_ssem.at[piece],
+            recv_sem=r1_rsem.at[source], device_id={"ctx": piece}, device_id_type=MESH,
+        )
+
+    def backward(step, _):
+        group, heads = group_of(step)
+        nq = HG // 2
+        qk = [group * nq + i for i in range(nq)]
+        q_piece = group * (nq // 2)
+        k_piece = BLOCKS // 4 + group * (nq // 2)
+        v_piece = BLOCKS // 2 + group * (HG // 2)
+        for h in heads:
+            @pl.when(h != me)
+            def _():
                 g_copy(h, h).wait_recv()
         packed = jnp.zeros((ROWS, D), F32)
         colsums, lasts = [], []
@@ -365,17 +419,12 @@
             for i in (2 * n, 2 * n + 1):
                 h = heads[i]
                 _, bet, car, end, bcar = columns(h)
-                s, g = s_rcv[h], g_rcv[h]
-                do = dcore_ref[:, lanes(h)]
-                t = dot(wq_s[h], s, 1, 1)
-                u = (uv_s[h] - t[:ROWS]).astype(BF)
-                core_ref[:, lanes(h)] = (ol_s[h] + t[ROWS:]).astype(BF)
+                s, g, u = s_rcv[h], g_rcv[h], u_s[h]
+                dos, dp = dos_s[h], dp_s[h]
                 r = r0_s[h] + dot(w2_s[h], g, 1, 1)
-                dr = jnp.concatenate([do, r.astype(BF)], axis=0)
-                t2 = dot(dr, s)
-                dos, rs = t2[:ROWS], t2[ROWS:]
-                t3 = dot(dr, u, 1, 1)
-                dp, da = t3[:ROWS], -t3[ROWS:]
+                rb = r.astype(BF)
+                rs = dot(rb, s)
+                da = -dot(rb, u, 1, 1)
                 ug = dot(u, g)
                 spans = d_s[h]
                 t1 = da * dkk_s[h]
@@ -386,8 +435,8 @@
                 dkug = end * k * ug
                 dbeta = jnp.sum(r * v - krs + t1, axis=1, keepdims=True)
                 dc = jnp.sum(f + car * q * dos - bet * krs - dkug, axis=1, keepdims=True)
-                packed = packed + jnp.where(lane == 2 * i, dc, 0.0)
-                packed = packed + jnp.where(lane == 2 * i + 1, dbeta, 0.0)
+                packed = packed + jnp.where(lane == i, dc, 0.0)
+                packed = packed + jnp.where(lane == HG + i, dbeta, 0.0)
                 colsums.append(jnp.sum(f, axis=0, keepdims=True))
                 lasts.append(
                     jnp.sum(
@@ -405,7 +454,7 @@
                 es = e if es is None else es + e
                 dq = dqi if dq is None else dq + dqi
                 dk = dki if dk is None else dk + dki
-                conv_back(2 * QK + h, bet * r)
+                conv_back(2 * QK + h, v_piece + i // 2, i % 2, bet * r)
             be = jnp.concatenate([bs, es], axis=0).astype(BF)
             kb = k.astype(BF)
             t4 = dot(be, kb)
@@ -416,19 +465,36 @@
             m = y / (1.0 + jnp.exp(-y))
             rq = lax.rsqrt(jnp.sum(m * m, axis=1, keepdims=True) + 1e-6)
             dm = rq * (D**-0.5) * (dq - m * (rq * rq * jnp.sum(m * dq, axis=1, keepdims=True)))
-            conv_back(j, dm)
+            conv_back(j, q_piece + n // 2, n % 2, dm)
             y = ys[:, lanes(QK + j)]
             m = y / (1.0 + jnp.exp(-y))
             rk = lax.rsqrt(jnp.sum(m * m, axis=1, keepdims=True) + 1e-6)
             dm = rk * (dk - m * (rk * rk * jnp.sum(m * dk, axis=1, keepdims=True)))
-            conv_back(QK + j, dm)
+            conv_back(QK + j, k_piece + n // 2, n % 2, dm)
         rows = jnp.transpose(packed)
-        lane1 = lane[:1]
-        for i, h in enumerate(heads):
-            dgt[0, pl.ds(h, 1), :] = (
-                rows[2 * i : 2 * i + 1] - colsums[i] + jnp.where(lane1 == D - 1, lasts[i], 0.0)
-            )
-            dgt[1, pl.ds(h, 1), :] = rows[2 * i + 1 : 2 * i + 2]
+        lasts = jnp.concatenate(lasts, axis=0)
+        dc = rows[:HG] - jnp.concatenate(colsums, axis=0)
+        dc = dc + jnp.where(lane[:HG] == D - 1, lasts, 0.0)
+        dg = dot_full(dc, suffix)
+        dz = dg * gts[1, group]
+        bet = gts[2, group]
+        dgo[0, group] = dz
+        dgo[1, group] = rows[HG : 2 * HG] * bet * (1.0 - bet)
+        sums = dot_full(jnp.ones((8, D), F32), jnp.concatenate([dg * gts[0, group], dz], axis=0), 1, 1)
+        red[q_piece, 4:5, 0 : 2 * HG] = sums[0:1]
+        pieces = (
+            [q_piece + i for i in range(nq // 2)]
+            + [k_piece + i for i in range(nq // 2)]
+            + [v_piece + i for i in range(HG // 2)]
+        )
+        for piece in pieces:
+            @pl.when(piece != me)
+            def _():
+                red_copy(piece, me).start()
+
+            @pl.when(piece == me)
+            def _():
+                r1[me] = red[piece]
         return 0
 
     lax.fori_loop(0, HEADS // HG, backward, 0)
@@ -445,15 +511,56 @@
     )
     back.start()
 
-    dg = dot_full(dgt[0], jnp.where(row >= col, 1.0, 0.0))
-    dz = dg * gts[1]
-    bet = gts[2]
-    both = jnp.concatenate([dz, dgt[1] * bet * (1.0 - bet)], axis=0)
-    dgate_ref[...] = dot_full(jnp.where(row == col, 1.0, 0.0), both, 1, 1)
-    ones = jnp.ones((1, D), F32)
-    red_ref[4:8, :] = jnp.zeros((4, CH), F32)
-    red_ref[4:5, 0:HEADS] = dot_full(ones, dg * gts[0], 1, 1)
-    red_ref[5:6, 0:HEADS] = dot_full(ones, dz, 1, 1)
+    def wait_red(i, _):
+        other = lax.rem(me + i, BLOCKS)
+        red_copy(other, other).wait_recv()
+        return 0
+
+    lax.fori_loop(1, BLOCKS, wait_red, 0)
+    total = r1[0]
+    for i in range(1, BLOCKS):
+        total = total + r1[i]
+    r2[mine] = total
+
+    def dp_copy(other, source):
+        return pltpu.make_async_remote_copy(
+            src_ref=r2.at[source], dst_ref=r2.at[source], send_sem=r2_ssem.at[other],
+            recv_sem=r2_rsem.at[source], device_id={"dp": other}, device_id_type=MESH,
+        )
+
+    def send_dp(i, _):
+        dp_copy(lax.rem(mine + i, DP), mine).start()
+        return 0
+
+    lax.fori_loop(1, DP, send_dp, 0)
+
+    for n in range(HEADS // HG):
+        part = slice(n * HG, n * HG + HG)
+        dgate_ref[part, :] = dgo[0, n]
+        dgate_ref[HEADS + n * HG : HEADS + n * HG + HG, :] = dgo[1, n]
+
+    def wait_dp(i, _):
+        other = lax.rem(mine + i, DP)
+        dp_copy(other, other).wait_recv()
+        return 0
+
+    lax.fori_loop(1, DP, wait_dp, 0)
+    total = r2[0]
+    for i in range(1, DP):
+        total = total + r2[i]
+    r3[me] = total
+
+    def all_copy(other, source):
+        return pltpu.make_async_remote_copy(
+            src_ref=r3.at[source], dst_ref=r3.at[source], send_sem=r3_ssem.at[other],
+            recv_sem=r3_rsem.at[source], device_id={"ctx": other}, device_id_type=MESH,
+        )
+
+    def send_all(i, _):
+        all_copy(lax.rem(me + i, BLOCKS), me).start()
+        return 0
+
+    lax.fori_loop(1, BLOCKS, send_all, 0)
 
     back.wait()
     before_last = jnp.where(me < BLOCKS - 1, 1.0, 0.0)
@@ -466,14 +573,36 @@
             [old[:8], part], axis=0
         ).astype(BF)
 
+    def wait_all(i, _):
+        other = lax.rem(me + i, BLOCKS)
+        all_copy(other, other).wait_recv()
+        return 0
+
+    lax.fori_loop(1, BLOCKS, wait_all, 0)
+    for p in range(BLOCKS):
+        dconv_ref[:, p * PIECE : (p + 1) * PIECE] = r3[p, 0:4]
+    for n in range(HEADS // HG):
+        part = slice(n * HG, n * HG + HG)
+        sums = r3[n * (HG // 4), 4:5]
+        dhead_ref[0:1, part] = sums[:, 0:HG]
+        dhead_ref[1:2, part] = sums[:, HG : 2 * HG]
+
     def drain(i, _):
         other = lax.rem(me + i, BLOCKS)
         pack_copy(other, me).wait_send()
         s_copy(other, me).wait_send()
         g_copy(other, me).wait_send()
+        red_copy(other, me).wait_send()
+        all_copy(other, me).wait_send()
         return 0
 
     lax.fori_loop(1, BLOCKS, drain, 0)
+
+    def drain_dp(i, _):
+        dp_copy(lax.rem(mine + i, DP), mine).wait_send()
+        return 0
+
+    lax.fori_loop(1, DP, drain_dp, 0)
 
 
 def on_device(mixed_in, conv_weight, gate_in, head_params, doc_lengths, d_core):
@@ -487,7 +616,7 @@
         pltpu.VMEM((3, ROWS, D), F32),
         pltpu.VMEM((ROWS, D), F32),
         pltpu.VMEM((HEADS, 8, D), F32),
-        pltpu.VMEM((3, HEADS, D), F32),
+        pltpu.VMEM((3, HEADS // HG, HG, D), F32),
         pltpu.VMEM(mat, F32),
         pltpu.VMEM(mat, F32),
         pltpu.VMEM(mat, F32),
@@ -507,7 +636,14 @@
         pltpu.VMEM((16, 1024), BF),
         pltpu.VMEM((16, CH), F32),
         pltpu.VMEM((16, 1024), BF),
-        pltpu.VMEM((2, HEADS, D), F32),
+        pltpu.VMEM((2, HEADS // HG, HG, D), F32),
+        pltpu.VMEM(mat, BF),
+        pltpu.VMEM(mat, F32),
+        pltpu.VMEM(mat, F32),
+        pltpu.VMEM((BLOCKS, 8, PIECE), F32),
+        pltpu.VMEM((BLOCKS, 8, PIECE), F32),
+        pltpu.VMEM((DP, 8, PIECE), F32),
+        pltpu.VMEM((BLOCKS, 8, PIECE), F32),
         pltpu.SemaphoreType.DMA((BLOCKS,)),
         pltpu.SemaphoreType.DMA((BLOCKS,)),
         pltpu.SemaphoreType.DMA((BLOCKS,)),
@@ -516,25 +652,31 @@
         pltpu.SemaphoreType.DMA((BLOCKS,)),
         pltpu.SemaphoreType.DMA((2,)),
         pltpu.SemaphoreType.DMA((2,)),
+        pltpu.SemaphoreType.DMA((BLOCKS,)),
+        pltpu.SemaphoreType.DMA((BLOCKS,)),
+        pltpu.SemaphoreType.DMA((DP,)),
+        pltpu.SemaphoreType.DMA((DP,)),
+        pltpu.SemaphoreType.DMA((BLOCKS,)),
+        pltpu.SemaphoreType.DMA((BLOCKS,)),
     ]
-    core, dmix, dgate, red = pl.pallas_call(
+    core, dmix, dgate, dconv, dhead = pl.pallas_call(
         kernel,
         out_shape=(
             jax.ShapeDtypeStruct((ROWS, HEADS * D), BF),
             jax.ShapeDtypeStruct((ROWS, CH), BF),
-            jax.ShapeDtypeStruct((ROWS, 2 * HEADS), F32),
-            jax.ShapeDtypeStruct((8, CH), F32),
+            jax.ShapeDtypeStruct((2 * HEADS, ROWS), F32),
+            jax.ShapeDtypeStruct((4, CH), F32),
+            jax.ShapeDtypeStruct((2, HEADS), F32),
         ),
         in_specs=[vmem, vmem, vmem, vmem, pl.BlockSpec(memory_space=pltpu.SMEM), vmem],
-        out_specs=(vmem, vmem, vmem, vmem),
+        out_specs=(vmem,) * 5,
         scratch_shapes=scratch,
         compiler_params=pltpu.CompilerParams(
             collective_id=0, has_side_effects=True, vmem_limit_bytes=56 * 1024 * 1024
         ),
         name="delta_mix",
-    )(mixed_in[0], conv_weight, gate_in[0], head_params, doc_lengths, d_core[0])
-    red = lax.psum(red, ("dp", "ctx"))
-    return core[None], dmix[None], dgate[None], red[:4], red[4:6, :HEADS]
+    )(mixed_in[0], conv_weight, gate_in[0].T, head_params, doc_lengths, d_core[0])
+    return core[None], dmix[None], dgate.T[None], dconv, dhead
 
 
 def solution(mesh):

time: 242 us -> 96.4 us (0.40)
  waiting for transfers between devices: 142 us -> 0 us
  Pallas kernels: 76.8 us -> 90.8 us
  between operations: 14 us -> 0.65 us
  local copies, waits for them, and re-layouts: 8.68 us -> 4.8 us
    psum x1 -> x0, waiting for transfers between devices: 142 us -> none  [on_device(): red = lax.psum(red, ('dp', 'ctx'))]
    pallas_call x1, Pallas kernels: 76.8 us -> 90.8 us  [on_device(): pl.pallas_call(kernel, out_shape=(jax.ShapeDtypeStruct((ROWS, HEADS * D),...]
    slice x2 -> x0, local copies, waits for them, and re-layouts: 2.77 us -> none  [on_device(): return (core[None], dmix[None], dgate[None], red[:4], red[4:6, :HEADS])]
    unnamed x6 -> x13, local copies, waits for them, and re-layouts: 5.9 us -> 4.8 us
  transfers between devices with their start and end apart: 1 -> 0, of which waited for: 1 -> 0; matrix products, arithmetic and copies ran while one was open for 1% -> 0% of each run, Pallas kernels for 0% -> 0%
where the time goes in v2:
time: 96.4 us; the launch traced here: 96.3 us
  Pallas kernels  90.8 us (94%)
  local copies, waits for them, and re-layouts  4.8 us (5%)
    pallas_call x1, Pallas kernels, on_device(): pl.pallas_call(kernel, out_shape=(jax.ShapeDtypeStruct((ROWS, HEADS * D),...  90.8 us
    unnamed x13, local copies, waits for them, and re-layouts  4.8 us

profile of v2, /device:TPU:1, one launch (start us, length us, event | category | flops | bytes accessed | tf_op | source)
XLA Modules:
  0.0 96.3 jit_solution(4721032577643761034)
XLA Ops:
  0.6 90.8 %delta_mix.1 = (bf16[128,2048]{1,0:T(8,128)(2,1)}, bf16[128,4096]{1,0:T(8,128)(2,1)}, f32[32,128]{1,0:T(8,128)}, f32[4,4096]{1,0:T(4,128)}, f32[2,16]{1,0:T(2,128)}) custom-call(bf16[128,4096]{1,0:T(8,128)(2,1)} %bitcast.10, f32[4,4096]{1,0:T(4,128)} %w_ref.1, f32[32,128]{1,0:T(8,128)} %bitcast.14, f32[2,16]{1,0:T(2,128)} %hp_ref.1, s32[1,8]{1,0:T(1,128)} %len_ref.1, ...), custom_call_target="tpu_custom_call" | custom-call | tf_op jit(solution)/shard_map/delta_mix/pallas_call | solution.py:662
  91.4 0.0 copy-start
  91.5 2.0 %copy.16 = bf16[1,128,2048]{2,1,0:T(8,128)(2,1)} copy(bf16[1,128,2048]{2,1,0:T(8,128)(2,1)} %bitcast.13) | data formatting | bytes 1048576
  93.4 0.0 copy-done
  93.4 0.0 copy-start.2
  93.4 0.0 copy-start.1
  93.4 1.0 %copy.17 = bf16[1,128,4096]{2,1,0:T(8,128)(2,1)} copy(bf16[1,128,4096]{2,1,0:T(8,128)(2,1)S(1)} %bitcast.11) | data formatting | bytes 2097152
  94.4 0.0 copy-done.2
  94.4 0.6 copy.18
  95.0 0.0 copy-done.1
  95.0 0.0 copy-start.3
  95.0 0.6 copy.19
  95.6 0.0 copy-done.3
  95.7 0.6 copy.20
Async XLA Ops:
  91.4 2.0 %copy-start = (bf16[128,4096]{1,0:T(8,128)(2,1)S(1)}, bf16[128,4096]{1,0:T(8,128)(2,1)}, u32[]{:S(2)}) copy-start(bf16[128,4096]{1,0:T(8,128)(2,1)} %get-tuple-element.11) | copy-start | bytes 3145732
  93.4 1.0 %copy-start.2 = (f32[32,128]{1,0:T(8,128)S(1)}, f32[32,128]{1,0:T(8,128)}, u32[]{:S(2)}) copy-start(f32[32,128]{1,0:T(8,128)} %get-tuple-element.12) | copy-start | bytes 49156
  93.4 1.6 %copy-start.1 = (f32[4,4096]{1,0:T(4,128)S(1)}, f32[4,4096]{1,0:T(4,128)}, u32[]{:S(2)}) copy-start(f32[4,4096]{1,0:T(4,128)} %get-tuple-element.23) | copy-start | bytes 196612
  95.0 0.7 copy-start.3

commit v3 on v2

--- a/solution.py
+++ b/solution.py
@@ -12,9 +12,8 @@
 CH = 4096
 BLOCKS = 16
 PACK = 3 * D + 16
-FG = 8
 HG = 4
-ASIDE = 2
+GROUPS = HEADS // HG
 DP = 8
 PIECE = CH // BLOCKS
 F32 = jnp.float32
@@ -75,11 +74,16 @@
     return xs
 
 
+def parts_of(group):
+    first, second = 4 * group, 4 * ((group + 2) % 4) + 2
+    return [(0, first, first + 2), (2, second, second + 2)]
+
+
 def kernel(
     x_ref, w_ref, gate_ref, hp_ref, len_ref, dcore_ref,
     core_ref, dmix_ref, dgate_ref, dconv_ref, dhead_ref,
-    xs, ys, qs, ks, links, lks, gt, gts, d_s, dkk_s, p_s, x_s, uv_s, wq_s, w2_s, r0_s, ol_s,
-    snd, rcv, s_snd, g_snd, s_rcv, g_rcv, h_snd, h_rcv, e_snd, e_rcv, dgo, u_s, dos_s, dp_s, red, r1, r2, r3,
+    xs, slope, qs, ks, norms, links, lks, gt, gts, d_s, dkk_s, p_s, x_s, uv_s, wq_s, w2_s, r0_s, ol_s,
+    snd, rcv, s_snd, g_snd, s_rcv, g_rcv, h_snd, h_rcv, e_add, e_rcv, dgo, u_s, a_s, v_s, b_s, e_s, ck_s, bck_s, bc_s, ek_s, end_s, dk_s, dcs, red, r1, r2, r3,
     snd_sem, rcv_sem, s_ssem, s_rsem, g_ssem, g_rsem, h_sem, e_sem,
     r1_ssem, r1_rsem, r2_ssem, r2_rsem, r3_ssem, r3_rsem,
 ):
@@ -87,6 +91,14 @@
     mine = lax.axis_index("dp")
     first_pos = me * ROWS
 
+    own_row = lax.div(me, 4)
+    own_pair = lax.rem(lax.div(me, 2), 2)
+
+    def group_of(step):
+        group = lax.rem(own_row + step + 2 * own_pair, 4)
+        qk = [2 * group, 2 * lax.rem(group + 2, 4) + 1]
+        return group, qk, [2 * j + i for j in qk for i in range(2)]
+
     barrier = pltpu.get_barrier_semaphore()
 
     def greet(i, _):
@@ -95,7 +107,7 @@
         )
         return 0
 
-    lax.fori_loop(1, BLOCKS, greet, 0)
+    lax.fori_loop(1, BLOCKS, greet, 0, unroll=True)
 
     def greet_dp(i, _):
         pl.semaphore_signal(
@@ -103,7 +115,7 @@
         )
         return 0
 
-    lax.fori_loop(1, DP, greet_dp, 0)
+    lax.fori_loop(1, DP, greet_dp, 0, unroll=True)
 
     xs[pl.ds(8, ROWS), :] = x_ref[...].astype(F32)
     tail = [
@@ -159,11 +171,11 @@
     to_end = jnp.exp(jnp.minimum(summed[:, D - 1 : D] - summed, 0.0)) * (
         doc_row16 == doc_last
     ).astype(F32)
-    for n in range(HEADS // HG):
-        part = slice(n * HG, n * HG + HG)
-        gts[0, n] = decay[part]
-        gts[1, n] = ez[part]
-        gts[2, n] = beta[part]
+    for n in range(GROUPS):
+        for at, a, b in parts_of(n):
+            gts[0, n, at : at + 2] = decay[a:b]
+            gts[1, n, at : at + 2] = ez[a:b]
+            gts[2, n, at : at + 2] = beta[a:b]
     rows8 = jnp.stack(
         [summed, beta, carried, to_end, beta * carried, summed, summed, summed], axis=1
     )
@@ -187,8 +199,10 @@
         y = taps(3, block) * w_ref[3:4, lanes(block)]
         for j in range(3):
             y = y + taps(j, block) * w_ref[j : j + 1, lanes(block)]
-        ys[:, lanes(block)] = y
-        return y / (1.0 + jnp.exp(-y))
+        sig = 1.0 / (1.0 + jnp.exp(-y))
+        m = y * sig
+        slope[:, lanes(block)] = sig + m * (1.0 - sig)
+        return m
 
     def columns(h):
         t = jnp.transpose(gt[h])
@@ -204,16 +218,17 @@
         )
 
     def forward(step, _):
-        group = lax.rem(step + me, HEADS // FG)
-        nq = FG // 2
-        qk = [group * nq + i for i in range(nq)]
-        heads = [group * FG + i for i in range(FG)]
+        _, qk, heads = group_of(step)
         kk, qq, kf, qf = [], [], [], []
         for j in qk:
             m = conv(j)
-            q = m * (lax.rsqrt(jnp.sum(m * m, axis=1, keepdims=True) + 1e-6) * D**-0.5)
+            norm = lax.rsqrt(jnp.sum(m * m, axis=1, keepdims=True) + 1e-6) * D**-0.5
+            norms[j] = jnp.broadcast_to(norm, (ROWS, D))
+            q = m * norm
             m = conv(QK + j)
-            k = m * lax.rsqrt(jnp.sum(m * m, axis=1, keepdims=True) + 1e-6)
+            norm = lax.rsqrt(jnp.sum(m * m, axis=1, keepdims=True) + 1e-6)
+            norms[QK + j] = jnp.broadcast_to(norm, (ROWS, D))
+            k = m * norm
             qs[j] = q
             ks[j] = k
             k2, q2 = split(k), split(q)
@@ -229,11 +244,14 @@
             spans = lk * jnp.exp(jnp.minimum(cols[i][0] - gt[h][0:1], 0.0))
             dkk = jnp.where(strict, spans * kk[i // 2], 0.0)
             p = spans * qq[i // 2]
+            mat = cols[i][1] * dkk
             d_s[h] = spans
             dkk_s[h] = dkk
+            a_s[h] = mat
             p_s[h] = p
+            v_s[h] = vs[i]
             ps.append(p.astype(BF))
-            mats.append(cols[i][1] * dkk)
+            mats.append(mat)
         xinv = inverses(mats)
         for i, h in enumerate(heads):
             x_s[h] = xinv[i]
@@ -266,7 +284,7 @@
                 pack_copy(h, me).start()
         return 0
 
-    lax.fori_loop(0, HEADS // FG, forward, 0)
+    lax.fori_loop(0, GROUPS, forward, 0)
     rcv[me] = snd[me]
 
     def aside(step, _):
@@ -274,19 +292,20 @@
         for i, h in enumerate(heads):
             cols = columns(h)
             zz = dot(p_s[h].astype(BF), dcore_ref[:, lanes(h)], 0, 0)
-            dk = cols[3] * ks[h // 2]
+            k = ks[h // 2]
+            dk = cols[3] * k
+            b_s[h] = jnp.broadcast_to(cols[1], (ROWS, D))
+            e_s[h] = jnp.where(strict, cols[1] * d_s[h], 0.0)
+            ck_s[h] = cols[2] * k
+            bck_s[h] = cols[4] * k
+            bc_s[h] = jnp.broadcast_to(cols[4], (ROWS, D))
+            ek_s[h] = dk
+            end_s[h] = jnp.broadcast_to(cols[3], (ROWS, D))
             out = dot3(split(x_s[h]), split(jnp.concatenate([zz, dk], axis=1)), 0, 0)
             r0_s[h] = out[:, :D]
             w2_s[h] = out[:, D:].astype(BF)
         return 0
 
-    lax.fori_loop(0, ASIDE, aside, 0)
-
-    def wait_pack(i, _):
-        pack_copy(lax.rem(me + i, BLOCKS), lax.rem(me + i, BLOCKS)).wait_recv()
-        return 0
-
-    lax.fori_loop(1, BLOCKS, wait_pack, 0)
 
     def s_copy(block, head):
         return pltpu.make_async_remote_copy(
@@ -300,15 +319,16 @@
             recv_sem=g_rsem.at[head], device_id={"ctx": block}, device_id_type=MESH,
         )
 
-    def send_state(block, state):
-        s_snd[block] = state
-
-        @pl.when(block != me)
-        def _():
-            s_copy(block, me).start()
+    lax.fori_loop(0, GROUPS, aside, 0)
+
+    def wait_pack(i, _):
+        pack_copy(lax.rem(me + i, BLOCKS), lax.rem(me + i, BLOCKS)).wait_recv()
+        return 0
+
+    lax.fori_loop(1, BLOCKS, wait_pack, 0, unroll=True)
 
     zero = jnp.zeros((D, D), F32)
-    send_state(0, zero.astype(BF))
+    s_snd[0] = zero.astype(BF)
     g_snd[BLOCKS - 1] = zero.astype(BF)
 
     def scalar_of(block):
@@ -328,85 +348,122 @@
             - dot(grad.astype(BF), rcv[b, 0:D], 1, 1)
             + rcv[b, 2 * D : 3 * D].astype(F32)
         )
-        send_state(i + 1, state.astype(BF))
+        s_snd[i + 1] = state.astype(BF)
         g_snd[b - 1] = grad.astype(BF)
         return state, grad
 
     lax.fori_loop(0, BLOCKS - 1, turn, (zero, zero))
 
+    def reader(i):
+        step, which = lax.div(i, 4), lax.rem(lax.div(i, 2), 2)
+        row = lax.rem(own_row + 8 - step - 2 * which, 4)
+        return 4 * row + 2 * lax.rem(own_pair + which, 2) + lax.rem(i, 2)
+
+    def send_state(i, _):
+        other = reader(i)
+
+        @pl.when(other != me)
+        def _():
+            s_copy(other, me).start()
+        return 0
+
+    lax.fori_loop(0, BLOCKS, send_state, 0, unroll=True)
+
     def send_grad(i, _):
-        other = lax.rem(me + i, BLOCKS)
-        g_copy(other, me).start()
-        return 0
-
-    lax.fori_loop(1, BLOCKS, send_grad, 0)
+        other = reader(i)
+
+        @pl.when(other != me)
+        def _():
+            g_copy(other, me).start()
+        return 0
+
+    lax.fori_loop(0, BLOCKS, send_grad, 0, unroll=True)
     s_rcv[me] = s_snd[me]
     g_rcv[me] = g_snd[me]
-    lax.fori_loop(ASIDE, HEADS // HG, aside, 0)
+
 
     lane = col
-    row8 = row[:8]
 
     def conv_back(block, piece, half, dm):
         at = pl.ds(half * D, D)
-        y = ys[:, lanes(block)]
-        sig = 1.0 / (1.0 + jnp.exp(-y))
-        dy = dm * (sig * (1.0 + y * (1.0 - sig)))
-        red[piece, 3:4, at] = jnp.sum(dy * taps(3, block), axis=0, keepdims=True)
+        dy = dm * slope[:, lanes(block)]
+        slope[:, lanes(block)] = dy
+        for j in range(4):
+            red[piece, j : j + 1, at] = jnp.sum(dy * taps(j, block), axis=0, keepdims=True)
+
+    def taps_back(block):
+        dy = slope[:, lanes(block)]
         own = dy * w_ref[3:4, lanes(block)]
-        spill = jnp.zeros((8, D), F32)
         for j in range(3):
-            ej = dy * links[j]
-            red[piece, j : j + 1, at] = jnp.sum(
-                ej * xs[pl.ds(5 + j, ROWS), lanes(block)], axis=0, keepdims=True
-            )
-            turned = pltpu.roll(ej * w_ref[j : j + 1, lanes(block)], ROWS - 3 + j, 0)
-            wrapped = row >= ROWS - 3 + j
-            own = own + jnp.where(wrapped, 0.0, turned)
-            spill = spill + jnp.where(row8 >= 5 + j, turned[ROWS - 8 :], 0.0)
-        dmix_ref[:, lanes(block)] = own.astype(BF)
-        e_snd[0:8, lanes(block)] = own[ROWS - 8 :]
-        e_snd[8:16, lanes(block)] = spill
-
-    def group_of(step):
-        group = lax.rem(step + me, HEADS // HG)
-        return group, [group * HG + i for i in range(HG)]
+            turned = pltpu.roll(dy * links[j] * w_ref[j : j + 1, lanes(block)], ROWS - 3 + j, 0)
+            own = own + jnp.where(row >= ROWS - 3 + j, 0.0, turned)
+        last = own[ROWS - 8 :] + e_add[:, lanes(block)]
+        dmix_ref[:, lanes(block)] = jnp.concatenate([own[: ROWS - 8], last], axis=0).astype(BF)
+
+    def results(step, _):
+        for i in range(HG):
+            h = step * HG + i
+            core_ref[:, lanes(h)] = (
+                ol_s[h] + dot(wq_s[h, ROWS : 2 * ROWS], s_rcv[h], 1, 1)
+            ).astype(BF)
+        return 0
+
+    suffix = jnp.where(row >= col, 1.0, 0.0)
+    red[:, 4:8, :] = jnp.zeros((BLOCKS, 4, PIECE), F32)
+
+    def red_copy(piece, source):
+        return pltpu.make_async_remote_copy(
+            src_ref=red.at[piece], dst_ref=r1.at[source], send_sem=r1_ssem.at[piece],
+            recv_sem=r1_rsem.at[source], device_id={"ctx": piece}, device_id_type=MESH,
+        )
+
+    def send_piece(piece):
+        @pl.when(piece != me)
+        def _():
+            red_copy(piece, me).start()
+
+        @pl.when(piece == me)
+        def _():
+            r1[me] = red[piece]
 
     def from_state(step, _):
-        _, heads = group_of(step)
+        group, qk, heads = group_of(step)
         for h in heads:
             @pl.when(h != me)
             def _():
                 s_copy(h, h).wait_recv()
-        for h in heads:
-            s = s_rcv[h]
-            do = dcore_ref[:, lanes(h)]
-            t = dot(wq_s[h], s, 1, 1)
-            u = (uv_s[h] - t[:ROWS]).astype(BF)
-            core_ref[:, lanes(h)] = (ol_s[h] + t[ROWS:]).astype(BF)
-            u_s[h] = u
-            dos_s[h] = dot(do, s)
-            dp_s[h] = dot(do, u, 1, 1)
-        return 0
-
-    lax.fori_loop(0, HEADS // HG, from_state, 0)
-
-    suffix = jnp.where(row >= col, 1.0, 0.0)
-    red[:, 4:8, :] = jnp.zeros((BLOCKS, 4, PIECE), F32)
-
-    def red_copy(piece, source):
-        return pltpu.make_async_remote_copy(
-            src_ref=red.at[piece], dst_ref=r1.at[source], send_sem=r1_ssem.at[piece],
-            recv_sem=r1_rsem.at[source], device_id={"ctx": piece}, device_id_type=MESH,
-        )
+        packed = jnp.zeros((ROWS, D), F32)
+        colsums = []
+        for n, j in enumerate(qk):
+            k, q = ks[j], qs[j]
+            bs = dq = None
+            for i in (2 * n, 2 * n + 1):
+                h = heads[i]
+                s = s_rcv[h]
+                do = dcore_ref[:, lanes(h)]
+                u = (uv_s[h] - dot(wq_s[h, 0:ROWS], s, 1, 1)).astype(BF)
+                u_s[h] = u
+                dos = columns(h)[2] * dot(do, s)
+                dp = dot(do, u, 1, 1)
+                f = dp * p_s[h]
+                packed = packed + jnp.where(
+                    lane == i, jnp.sum(f + q * dos, axis=1, keepdims=True), 0.0
+                )
+                colsums.append(jnp.sum(f, axis=0, keepdims=True))
+                bq = dp * d_s[h]
+                bs = bq if bs is None else bs + bq
+                dq = dos if dq is None else dq + dos
+            bs = bs.astype(BF)
+            dq = dq + dot(bs, k.astype(BF))
+            dk_s[j] = dot(bs, q.astype(BF), 0, 0)
+            dm = norms[j] * (dq - q * (D * jnp.sum(q * dq, axis=1, keepdims=True)))
+            conv_back(j, group, n, dm)
+        dcs[group] = jnp.transpose(packed)[:HG] - jnp.concatenate(colsums, axis=0)
+        return 0
 
     def backward(step, _):
-        group, heads = group_of(step)
-        nq = HG // 2
-        qk = [group * nq + i for i in range(nq)]
-        q_piece = group * (nq // 2)
-        k_piece = BLOCKS // 4 + group * (nq // 2)
-        v_piece = BLOCKS // 2 + group * (HG // 2)
+        group, qk, heads = group_of(step)
+        q_piece, k_piece, v_piece = group, GROUPS + group, 2 * (GROUPS + group)
         for h in heads:
             @pl.when(h != me)
             def _():
@@ -414,66 +471,43 @@
         packed = jnp.zeros((ROWS, D), F32)
         colsums, lasts = [], []
         for n, j in enumerate(qk):
-            k, q = ks[j], qs[j]
-            bs = es = dq = dk = None
+            k = ks[j]
+            es, dk = None, dk_s[j]
             for i in (2 * n, 2 * n + 1):
                 h = heads[i]
-                _, bet, car, end, bcar = columns(h)
                 s, g, u = s_rcv[h], g_rcv[h], u_s[h]
-                dos, dp = dos_s[h], dp_s[h]
                 r = r0_s[h] + dot(w2_s[h], g, 1, 1)
                 rb = r.astype(BF)
                 rs = dot(rb, s)
                 da = -dot(rb, u, 1, 1)
                 ug = dot(u, g)
-                spans = d_s[h]
-                t1 = da * dkk_s[h]
-                f = dp * p_s[h] + bet * t1
-                yv = ys[:, lanes(2 * QK + h)]
-                v = yv / (1.0 + jnp.exp(-yv))
-                krs = car * k * rs
-                dkug = end * k * ug
-                dbeta = jnp.sum(r * v - krs + t1, axis=1, keepdims=True)
-                dc = jnp.sum(f + car * q * dos - bet * krs - dkug, axis=1, keepdims=True)
+                f = da * a_s[h]
+                kug = ek_s[h] * ug
+                dbeta = jnp.sum(r * v_s[h] - ck_s[h] * rs + da * dkk_s[h], axis=1, keepdims=True)
+                dc = jnp.sum(f - bck_s[h] * rs - kug, axis=1, keepdims=True)
                 packed = packed + jnp.where(lane == i, dc, 0.0)
                 packed = packed + jnp.where(lane == HG + i, dbeta, 0.0)
                 colsums.append(jnp.sum(f, axis=0, keepdims=True))
                 lasts.append(
                     jnp.sum(
-                        jnp.sum(dkug, axis=0, keepdims=True)
+                        jnp.sum(kug, axis=0, keepdims=True)
                         + a_last(h)
                         * jnp.sum(g.astype(F32) * s.astype(F32), axis=0, keepdims=True),
                         axis=1, keepdims=True,
                     )
                 )
-                bq = dp * spans
-                e = jnp.where(strict, bet * da * spans, 0.0)
-                dqi = car * dos
-                dki = end * ug - bcar * rs
-                bs = bq if bs is None else bs + bq
+                e = da * e_s[h]
                 es = e if es is None else es + e
-                dq = dqi if dq is None else dq + dqi
-                dk = dki if dk is None else dk + dki
-                conv_back(2 * QK + h, v_piece + i // 2, i % 2, bet * r)
-            be = jnp.concatenate([bs, es], axis=0).astype(BF)
+                dk = dk + end_s[h] * ug - bc_s[h] * rs
+                conv_back(2 * QK + h, v_piece + i // 2, i % 2, b_s[h] * r)
+            es = es.astype(BF)
             kb = k.astype(BF)
-            t4 = dot(be, kb)
-            t5 = dot(be, jnp.concatenate([q.astype(BF), kb], axis=0), 0, 0)
-            dq = dq + t4[:ROWS]
-            dk = dk + t4[ROWS:] + t5
-            y = ys[:, lanes(j)]
-            m = y / (1.0 + jnp.exp(-y))
-            rq = lax.rsqrt(jnp.sum(m * m, axis=1, keepdims=True) + 1e-6)
-            dm = rq * (D**-0.5) * (dq - m * (rq * rq * jnp.sum(m * dq, axis=1, keepdims=True)))
-            conv_back(j, q_piece + n // 2, n % 2, dm)
-            y = ys[:, lanes(QK + j)]
-            m = y / (1.0 + jnp.exp(-y))
-            rk = lax.rsqrt(jnp.sum(m * m, axis=1, keepdims=True) + 1e-6)
-            dm = rk * (dk - m * (rk * rk * jnp.sum(m * dk, axis=1, keepdims=True)))
-            conv_back(QK + j, k_piece + n // 2, n % 2, dm)
+            dk = dk + dot(es, kb) + dot(es, kb, 0, 0)
+            dm = norms[QK + j] * (dk - k * jnp.sum(k * dk, axis=1, keepdims=True))
+            conv_back(QK + j, k_piece, n, dm)
         rows = jnp.transpose(packed)
         lasts = jnp.concatenate(lasts, axis=0)
-        dc = rows[:HG] - jnp.concatenate(colsums, axis=0)
+        dc = rows[:HG] - jnp.concatenate(colsums, axis=0) + dcs[group]
         dc = dc + jnp.where(lane[:HG] == D - 1, lasts, 0.0)
         dg = dot_full(dc, suffix)
         dz = dg * gts[1, group]
@@ -482,24 +516,20 @@
         dgo[1, group] = rows[HG : 2 * HG] * bet * (1.0 - bet)
         sums = dot_full(jnp.ones((8, D), F32), jnp.concatenate([dg * gts[0, group], dz], axis=0), 1, 1)
         red[q_piece, 4:5, 0 : 2 * HG] = sums[0:1]
-        pieces = (
-            [q_piece + i for i in range(nq // 2)]
-            + [k_piece + i for i in range(nq // 2)]
-            + [v_piece + i for i in range(HG // 2)]
-        )
-        for piece in pieces:
-            @pl.when(piece != me)
-            def _():
-                red_copy(piece, me).start()
-
-            @pl.when(piece == me)
-            def _():
-                r1[me] = red[piece]
-        return 0
-
-    lax.fori_loop(0, HEADS // HG, backward, 0)
-
-    spill = e_snd[8:16, :]
+        for piece in (q_piece, k_piece, v_piece, v_piece + 1):
+            send_piece(piece)
+        return 0
+
+    lax.fori_loop(0, GROUPS, from_state, 0)
+    lax.fori_loop(0, GROUPS, results, 0)
+    lax.fori_loop(0, GROUPS, backward, 0)
+
+    spill = jnp.zeros((8, CH), F32)
+    row8w = iota((8, CH), 0)
+    for j in range(3):
+        link8 = jnp.concatenate([links[j, 0:8]] * (CH // D), axis=1)
+        turned = pltpu.roll(slope[0:8, :] * link8 * w_ref[j : j + 1, :], 5 + j, 0)
+        spill = spill + jnp.where(row8w >= 5 + j, turned, 0.0)
     h_snd[...] = jnp.concatenate(
         [spill[5 + r : 6 + r, 1024 * p : 1024 * p + 1024] for r in range(3) for p in range(4)]
         + [jnp.zeros((4, 1024), F32)],
@@ -516,7 +546,7 @@
         red_copy(other, other).wait_recv()
         return 0
 
-    lax.fori_loop(1, BLOCKS, wait_red, 0)
+    lax.fori_loop(1, BLOCKS, wait_red, 0, unroll=True)
     total = r1[0]
     for i in range(1, BLOCKS):
         total = total + r1[i]
@@ -532,19 +562,34 @@
         dp_copy(lax.rem(mine + i, DP), mine).start()
         return 0
 
-    lax.fori_loop(1, DP, send_dp, 0)
-
-    for n in range(HEADS // HG):
-        part = slice(n * HG, n * HG + HG)
-        dgate_ref[part, :] = dgo[0, n]
-        dgate_ref[HEADS + n * HG : HEADS + n * HG + HG, :] = dgo[1, n]
+    lax.fori_loop(1, DP, send_dp, 0, unroll=True)
+
+    back.wait()
+    before_last = jnp.where(me < BLOCKS - 1, 1.0, 0.0)
+    ev = e_rcv[...].astype(F32) * before_last
+    for p in range(4):
+        e_add[:, 1024 * p : 1024 * p + 1024] = jnp.concatenate(
+            [jnp.zeros((5, 1024), F32)] + [ev[4 * r + p : 4 * r + p + 1] for r in range(3)], axis=0
+        )
+
+    def mixed_part(step, _):
+        for i in range(4):
+            taps_back(4 * step + i)
+        return 0
+
+    lax.fori_loop(0, 4, mixed_part, 0)
+
+    for n in range(GROUPS):
+        for at, a, b in parts_of(n):
+            dgate_ref[a:b, :] = dgo[0, n, at : at + 2]
+            dgate_ref[HEADS + a : HEADS + b, :] = dgo[1, n, at : at + 2]
 
     def wait_dp(i, _):
         other = lax.rem(mine + i, DP)
         dp_copy(other, other).wait_recv()
         return 0
 
-    lax.fori_loop(1, DP, wait_dp, 0)
+    lax.fori_loop(1, DP, wait_dp, 0, unroll=True)
     total = r2[0]
     for i in range(1, DP):
         total = total + r2[i]
@@ -560,32 +605,8 @@
         all_copy(lax.rem(me + i, BLOCKS), me).start()
         return 0
 
-    lax.fori_loop(1, BLOCKS, send_all, 0)
-
-    back.wait()
-    before_last = jnp.where(me < BLOCKS - 1, 1.0, 0.0)
-    ev = e_rcv[...].astype(F32) * before_last
-    for p in range(4):
-        pieces = [jnp.zeros((5, 1024), F32)] + [ev[4 * r + p : 4 * r + p + 1] for r in range(3)]
-        part = e_snd[0:8, 1024 * p : 1024 * p + 1024] + jnp.concatenate(pieces, axis=0)
-        old = dmix_ref[ROWS - 16 :, 1024 * p : 1024 * p + 1024].astype(F32)
-        dmix_ref[ROWS - 16 :, 1024 * p : 1024 * p + 1024] = jnp.concatenate(
-            [old[:8], part], axis=0
-        ).astype(BF)
-
-    def wait_all(i, _):
-        other = lax.rem(me + i, BLOCKS)
-        all_copy(other, other).wait_recv()
-        return 0
-
-    lax.fori_loop(1, BLOCKS, wait_all, 0)
-    for p in range(BLOCKS):
-        dconv_ref[:, p * PIECE : (p + 1) * PIECE] = r3[p, 0:4]
-    for n in range(HEADS // HG):
-        part = slice(n * HG, n * HG + HG)
-        sums = r3[n * (HG // 4), 4:5]
-        dhead_ref[0:1, part] = sums[:, 0:HG]
-        dhead_ref[1:2, part] = sums[:, HG : 2 * HG]
+    lax.fori_loop(1, BLOCKS, send_all, 0, unroll=True)
+    lax.fori_loop(4, 8, mixed_part, 0)
 
     def drain(i, _):
         other = lax.rem(me + i, BLOCKS)
@@ -593,16 +614,53 @@
         s_copy(other, me).wait_send()
         g_copy(other, me).wait_send()
         red_copy(other, me).wait_send()
-        all_copy(other, me).wait_send()
-        return 0
-
-    lax.fori_loop(1, BLOCKS, drain, 0)
+        return 0
+
+    lax.fori_loop(1, BLOCKS, drain, 0, unroll=True)
 
     def drain_dp(i, _):
         dp_copy(lax.rem(mine + i, DP), mine).wait_send()
         return 0
 
-    lax.fori_loop(1, DP, drain_dp, 0)
+    lax.fori_loop(1, DP, drain_dp, 0, unroll=True)
+
+    def wait_all(i, _):
+        other = lax.rem(me + i, BLOCKS)
+        all_copy(other, other).wait_recv()
+        return 0
+
+    lax.fori_loop(1, BLOCKS, wait_all, 0, unroll=True)
+    for n in range(GROUPS):
+        sums = r3[n, 4:5]
+        for at, a, b in parts_of(n):
+            lo = (at // 2) * D
+            dconv_ref[:, a // 2 * D : a // 2 * D + D] = r3[n, 0:4, lo : lo + D]
+            dconv_ref[:, (QK + a // 2) * D : (QK + a // 2 + 1) * D] = r3[GROUPS + n, 0:4, lo : lo + D]
+            dconv_ref[:, (2 * QK + a) * D : (2 * QK + b) * D] = r3[2 * (GROUPS + n) + at // 2, 0:4]
+            dhead_ref[0:1, a:b] = sums[:, at : at + 2]
+            dhead_ref[1:2, a:b] = sums[:, HG + at : HG + at + 2]
+
+    def drain_all(i, _):
+        all_copy(lax.rem(me + i, BLOCKS), me).wait_send()
+        return 0
+
+    lax.fori_loop(1, BLOCKS, drain_all, 0, unroll=True)
+
+
+def hand_on_kernel(*refs):
+    n = len(refs) // 2
+    for i in range(n):
+        refs[n + i][...] = refs[i][...]
+
+
+def hand_on(*arrays):
+    return pl.pallas_call(
+        hand_on_kernel,
+        out_shape=tuple(jax.ShapeDtypeStruct(a.shape, a.dtype) for a in arrays),
+        in_specs=[pl.BlockSpec(memory_space=pltpu.VMEM)] * len(arrays),
+        out_specs=(pl.BlockSpec(memory_space=pltpu.VMEM),) * len(arrays),
+        name="hand_on",
+    )(*arrays)
 
 
 def on_device(mixed_in, conv_weight, gate_in, head_params, doc_lengths, d_core):
@@ -613,10 +671,11 @@
         pltpu.VMEM((ROWS, CH), F32),
         pltpu.VMEM((QK, D, D), F32),
         pltpu.VMEM((QK, D, D), F32),
+        pltpu.VMEM((2 * QK, D, D), F32),
         pltpu.VMEM((3, ROWS, D), F32),
         pltpu.VMEM((ROWS, D), F32),
         pltpu.VMEM((HEADS, 8, D), F32),
-        pltpu.VMEM((3, HEADS // HG, HG, D), F32),
+        pltpu.VMEM((3, GROUPS, HG, D), F32),
         pltpu.VMEM(mat, F32),
         pltpu.VMEM(mat, F32),
         pltpu.VMEM(mat, F32),
@@ -634,12 +693,21 @@
         pltpu.VMEM(mat, BF),
         pltpu.VMEM((16, 1024), BF),
         pltpu.VMEM((16, 1024), BF),
-        pltpu.VMEM((16, CH), F32),
+        pltpu.VMEM((8, CH), F32),
         pltpu.VMEM((16, 1024), BF),
-        pltpu.VMEM((2, HEADS // HG, HG, D), F32),
+        pltpu.VMEM((2, GROUPS, HG, D), F32),
         pltpu.VMEM(mat, BF),
         pltpu.VMEM(mat, F32),
         pltpu.VMEM(mat, F32),
+        pltpu.VMEM(mat, F32),
+        pltpu.VMEM(mat, F32),
+        pltpu.VMEM(mat, F32),
+        pltpu.VMEM(mat, F32),
+        pltpu.VMEM(mat, F32),
+        pltpu.VMEM(mat, F32),
+        pltpu.VMEM(mat, F32),
+        pltpu.VMEM((QK, D, D), F32),
+        pltpu.VMEM((GROUPS, HG, D), F32),
         pltpu.VMEM((BLOCKS, 8, PIECE), F32),
         pltpu.VMEM((BLOCKS, 8, PIECE), F32),
         pltpu.VMEM((DP, 8, PIECE), F32),
@@ -676,6 +744,7 @@
         ),
         name="delta_mix",
     )(mixed_in[0], conv_weight, gate_in[0].T, head_params, doc_lengths, d_core[0])
+    core, dmix, dgate, dconv, dhead = hand_on(core, dmix, dgate, dconv, dhead)
     return core[None], dmix[None], dgate.T[None], dconv, dhead
 
 

time: 96.4 us -> 80 us (0.83)
  Pallas kernels: 90.8 us -> 79.2 us
  local copies, waits for them, and re-layouts: 4.8 us -> 0 us
    pallas_call x1, Pallas kernels: 90.8 us -> 76.5 us  [on_device(): pl.pallas_call(kernel, out_shape=(jax.ShapeDtypeStruct((ROWS, HEADS * D),...]
    unnamed x13 -> x0, local copies, waits for them, and re-layouts: 4.8 us -> none
    pallas_call x0 -> x1, Pallas kernels: none -> 2.61 us  [hand_on(): pl.pallas_call(hand_on_kernel, out_shape=tuple((jax.ShapeDtypeStruct(a.sh...]
where the time goes in v3:
time: 80 us; the launch traced here: 79.8 us
  Pallas kernels  79.2 us (99%)
    pallas_call x1, Pallas kernels, on_device(): pl.pallas_call(kernel, out_shape=(jax.ShapeDtypeStruct((ROWS, HEADS * D),...  76.5 us
    pallas_call x1, Pallas kernels, hand_on(): pl.pallas_call(hand_on_kernel, out_shape=tuple((jax.ShapeDtypeStruct(a.sh...  2.61 us

profile of v3, /device:TPU:1, one launch (start us, length us, event | category | flops | bytes accessed | tf_op | source)
XLA Modules:
  0.0 79.8 jit_solution(861009776010099765)
XLA Ops:
  0.6 76.5 %delta_mix.1 = (bf16[128,2048]{1,0:T(8,128)(2,1)}, bf16[128,4096]{1,0:T(8,128)(2,1)}, f32[32,128]{1,0:T(8,128)}, f32[4,4096]{1,0:T(4,128)}, f32[2,16]{1,0:T(2,128)}) custom-call(bf16[128,4096]{1,0:T(8,128)(2,1)} %bitcast.10, f32[4,4096]{1,0:T(4,128)} %w_ref.1, f32[32,128]{1,0:T(8,128)} %bitcast.12, f32[2,16]{1,0:T(2,128)} %hp_ref.1, s32[1,8]{1,0:T(1,128)} %len_ref.1, ...), custom_call_target="tpu_custom_call" | custom-call | tf_op jit(solution)/shard_map/delta_mix/pallas_call | solution.py:730
  77.2 2.6 %hand_on.1 = (bf16[128,2048]{1,0:T(8,128)(2,1)}, bf16[128,4096]{1,0:T(8,128)(2,1)}, f32[32,128]{1,0:T(8,128)}, f32[4,4096]{1,0:T(4,128)}, f32[2,16]{1,0:T(2,128)}) custom-call(bf16[128,2048]{1,0:T(8,128)(2,1)} %get-tuple-element.15.refs_0_, bf16[128,4096]{1,0:T(8,128)(2,1)} %get-tuple-element.16.refs_1_, f32[32,128]{1,0:T(8,128)} %get-tuple-element.17.refs_2_, ...), custom_call_target="tpu_custom_call" | custom-call | tf_op jit(solution)/shard_map/hand_on/pallas_call | solution.py:657

commit v4 on v3

--- a/solution.py
+++ b/solution.py
@@ -11,7 +11,7 @@
 ROWS = 128
 CH = 4096
 BLOCKS = 16
-PACK = 3 * D + 16
+PACK = 2 * D + 16
 HG = 4
 GROUPS = HEADS // HG
 DP = 8
@@ -80,17 +80,21 @@
 
 
 def kernel(
-    x_ref, w_ref, gate_ref, hp_ref, len_ref, dcore_ref,
-    core_ref, dmix_ref, dgate_ref, dconv_ref, dhead_ref,
-    xs, slope, qs, ks, norms, links, lks, gt, gts, d_s, dkk_s, p_s, x_s, uv_s, wq_s, w2_s, r0_s, ol_s,
-    snd, rcv, s_snd, g_snd, s_rcv, g_rcv, h_snd, h_rcv, e_add, e_rcv, dgo, u_s, a_s, v_s, b_s, e_s, ck_s, bck_s, bc_s, ek_s, end_s, dk_s, dcs, red, r1, r2, r3,
-    snd_sem, rcv_sem, s_ssem, s_rsem, g_ssem, g_rsem, h_sem, e_sem,
+    x_hbm, w_ref, gate_ref, hp_ref, len_ref, dcore_hbm,
+    core_hbm, dmix_hbm, dgate_ref, dconv_ref, dhead_ref,
+    x_ref, dcore_ref, core_ref, dmix_ref, io_sem, xs, slope, qs, ks, norms, links, lks, gt, gts, d_s, dkk_s, p_s, x_s, uv_s, wq_s, w2_s, r0_s, ol_s,
+    snd, rcv, snd2, rcv2, s_snd, g_snd, s_rcv, g_rcv, h_snd, h_rcv, e_add, e_rcv, dgo, u_s, a_s, v_s, b_s, e_s, ck_s, bck_s, bc_s, ek_s, end_s, dk_s, dcs, red, r1, r2, r3,
+    snd_sem, rcv_sem, snd2_sem, rcv2_sem, s_ssem, s_rsem, g_ssem, g_rsem, h_sem, e_sem,
     r1_ssem, r1_rsem, r2_ssem, r2_rsem, r3_ssem, r3_rsem,
 ):
     me = lax.axis_index("ctx")
     mine = lax.axis_index("dp")
     first_pos = me * ROWS
 
+    x_copy = pltpu.make_async_copy(x_hbm, x_ref, io_sem.at[0])
+    dcore_copy = pltpu.make_async_copy(dcore_hbm, dcore_ref, io_sem.at[1])
+    x_copy.start()
+    dcore_copy.start()
     own_row = lax.div(me, 4)
     own_pair = lax.rem(lax.div(me, 2), 2)
 
@@ -117,7 +121,9 @@
 
     lax.fori_loop(1, DP, greet_dp, 0, unroll=True)
 
+    x_copy.wait()
     xs[pl.ds(8, ROWS), :] = x_ref[...].astype(F32)
+    xs[0:8, :] = jnp.zeros((8, CH), F32)
     tail = [
         xs[pl.ds(133 + r, 1), pl.ds(1024 * p, 1024)] for r in range(3) for p in range(4)
     ] + [jnp.zeros((4, 1024), F32)]
@@ -156,6 +162,31 @@
     doc_row16 = doc_row[:HEADS]
     doc_before = doc_of(jnp.full((HEADS, D), first_pos - 1, jnp.int32))
     doc_last = doc_of(jnp.full((HEADS, D), first_pos + ROWS - 1, jnp.int32))
+
+    def lanes(block):
+        return pl.ds(pl.multiple_of(block * D, D), D)
+
+    def taps(j, block):
+        t = xs[pl.ds(5 + j, ROWS), lanes(block)]
+        return t if j == 3 else t * links[j]
+
+    def conv_first(step, _):
+        for i in range(4):
+            block = 4 * step + i
+            y = taps(3, block) * w_ref[3:4, lanes(block)]
+            for j in range(3):
+                y = y + taps(j, block) * w_ref[j : j + 1, lanes(block)]
+            slope[:, lanes(block)] = y
+        return 0
+
+    lax.fori_loop(0, 8, conv_first, 0)
+
+    def conv(block):
+        y = slope[:, lanes(block)]
+        sig = 1.0 / (1.0 + jnp.exp(-y))
+        m = y * sig
+        slope[:, lanes(block)] = sig + m * (1.0 - sig)
+        return m
 
     eye16 = (iota((16, 16), 0) == iota((16, 16), 1)).astype(F32)
     gates = gate_ref[...]
@@ -187,22 +218,13 @@
     for r in range(3):
         for p in range(4):
             xs[pl.ds(5 + r, 1), pl.ds(1024 * p, 1024)] = hv[4 * r + p : 4 * r + p + 1]
-
-    def lanes(block):
-        return pl.ds(pl.multiple_of(block * D, D), D)
-
-    def taps(j, block):
-        t = xs[pl.ds(5 + j, ROWS), lanes(block)]
-        return t if j == 3 else t * links[j]
-
-    def conv(block):
-        y = taps(3, block) * w_ref[3:4, lanes(block)]
-        for j in range(3):
-            y = y + taps(j, block) * w_ref[j : j + 1, lanes(block)]
-        sig = 1.0 / (1.0 + jnp.exp(-y))
-        m = y * sig
-        slope[:, lanes(block)] = sig + m * (1.0 - sig)
-        return m
+    y8 = xs[8:16, :] * w_ref[3:4, :]
+    for j in range(3):
+        link8 = jnp.concatenate([links[j, 0:8]] * (CH // D), axis=1)
+        y8 = y8 + xs[5 + j : 13 + j, :] * link8 * w_ref[j : j + 1, :]
+    slope[0:8, :] = y8
+    dcore_copy.wait()
+
 
     def columns(h):
         t = jnp.transpose(gt[h])
@@ -216,6 +238,18 @@
             src_ref=snd.at[h], dst_ref=rcv.at[source], send_sem=snd_sem.at[h],
             recv_sem=rcv_sem.at[source], device_id={"ctx": h}, device_id_type=MESH,
         )
+
+    def grad_pack_copy(h, source):
+        return pltpu.make_async_remote_copy(
+            src_ref=snd2.at[h], dst_ref=rcv2.at[source], send_sem=snd2_sem.at[h],
+            recv_sem=rcv2_sem.at[source], device_id={"ctx": h}, device_id_type=MESH,
+        )
+
+    def send_grad_packs(step):
+        for h in group_of(step)[2]:
+            @pl.when(h != me)
+            def _():
+                grad_pack_copy(h, me).start()
 
     def forward(step, _):
         _, qk, heads = group_of(step)
@@ -269,13 +303,13 @@
             gl = dot(dcore_ref[:, lanes(h)], qc, 0, 0)
             snd[h, 0:D] = nb[D:].astype(BF)
             snd[h, D : 2 * D] = nb[:D].astype(BF)
-            snd[h, 2 * D : 3 * D] = gl.astype(BF)
+            snd2[h] = gl.astype(BF)
             al = jnp.broadcast_to(a_last(h), (16, D))
             t0 = al.astype(BF).astype(F32)
             t1 = (al - t0).astype(BF).astype(F32)
             t2 = al - t0 - t1
             r16 = iota((16, D), 0)
-            snd[h, 3 * D : PACK] = jnp.where(
+            snd[h, 2 * D : PACK] = jnp.where(
                 r16 == 0, t0, jnp.where(r16 == 1, t1, jnp.where(r16 == 2, t2, 0.0))
             ).astype(BF)
         for h in heads:
@@ -285,7 +319,10 @@
         return 0
 
     lax.fori_loop(0, GROUPS, forward, 0)
+    for n in range(GROUPS):
+        send_grad_packs(n)
     rcv[me] = snd[me]
+    rcv2[me] = snd2[me]
 
     def aside(step, _):
         heads = [step * HG + i for i in range(HG)]
@@ -332,27 +369,19 @@
     g_snd[BLOCKS - 1] = zero.astype(BF)
 
     def scalar_of(block):
-        t = rcv[block, 3 * D : PACK].astype(F32)
+        t = rcv[block, 2 * D : PACK].astype(F32)
         return t[0:1] + t[1:2] + t[2:3]
 
-    def turn(i, carry):
-        state, grad = carry
-        b = BLOCKS - 1 - i
+    def turn(i, state):
         state = (
             scalar_of(i) * state
             - dot(state.astype(BF), rcv[i, 0:D])
             + rcv[i, D : 2 * D].astype(F32)
         )
-        grad = (
-            scalar_of(b) * grad
-            - dot(grad.astype(BF), rcv[b, 0:D], 1, 1)
-            + rcv[b, 2 * D : 3 * D].astype(F32)
-        )
         s_snd[i + 1] = state.astype(BF)
-        g_snd[b - 1] = grad.astype(BF)
-        return state, grad
-
-    lax.fori_loop(0, BLOCKS - 1, turn, (zero, zero))
+        return state
+
+    lax.fori_loop(0, BLOCKS - 1, turn, zero, unroll=True)
 
     def reader(i):
         step, which = lax.div(i, 4), lax.rem(lax.div(i, 2), 2)
@@ -368,6 +397,25 @@
         return 0
 
     lax.fori_loop(0, BLOCKS, send_state, 0, unroll=True)
+
+    def wait_grad_pack(i, _):
+        other = lax.rem(me + i, BLOCKS)
+        grad_pack_copy(other, other).wait_recv()
+        return 0
+
+    lax.fori_loop(1, BLOCKS, wait_grad_pack, 0, unroll=True)
+
+    def turn_back(i, grad):
+        b = BLOCKS - 1 - i
+        grad = (
+            scalar_of(b) * grad
+            - dot(grad.astype(BF), rcv[b, 0:D], 1, 1)
+            + rcv2[b].astype(F32)
+        )
+        g_snd[b - 1] = grad.astype(BF)
+        return grad
+
+    lax.fori_loop(0, BLOCKS - 1, turn_back, zero, unroll=True)
 
     def send_grad(i, _):
         other = reader(i)
@@ -522,6 +570,8 @@
 
     lax.fori_loop(0, GROUPS, from_state, 0)
     lax.fori_loop(0, GROUPS, results, 0)
+    core_copy = pltpu.make_async_copy(core_ref, core_hbm, io_sem.at[2])
+    core_copy.start()
     lax.fori_loop(0, GROUPS, backward, 0)
 
     spill = jnp.zeros((8, CH), F32)
@@ -579,6 +629,14 @@
 
     lax.fori_loop(0, 4, mixed_part, 0)
 
+    def mixed_copy(half):
+        part = pl.ds(half * (CH // 2), CH // 2)
+        return pltpu.make_async_copy(
+            dmix_ref.at[:, part], dmix_hbm.at[:, part], io_sem.at[3 + half]
+        )
+
+    mixed_copy(0).start()
+
     for n in range(GROUPS):
         for at, a, b in parts_of(n):
             dgate_ref[a:b, :] = dgo[0, n, at : at + 2]
@@ -607,10 +665,12 @@
 
     lax.fori_loop(1, BLOCKS, send_all, 0, unroll=True)
     lax.fori_loop(4, 8, mixed_part, 0)
+    mixed_copy(1).start()
 
     def drain(i, _):
         other = lax.rem(me + i, BLOCKS)
         pack_copy(other, me).wait_send()
+        grad_pack_copy(other, me).wait_send()
         s_copy(other, me).wait_send()
         g_copy(other, me).wait_send()
         red_copy(other, me).wait_send()
@@ -645,6 +705,9 @@
         return 0
 
     lax.fori_loop(1, BLOCKS, drain_all, 0, unroll=True)
+    core_copy.wait()
+    mixed_copy(0).wait()
+    mixed_copy(1).wait()
 
 
 def hand_on_kernel(*refs):
@@ -665,8 +728,14 @@
 
 def on_device(mixed_in, conv_weight, gate_in, head_params, doc_lengths, d_core):
     vmem = pl.BlockSpec(memory_space=pltpu.VMEM)
+    any_ = pl.BlockSpec(memory_space=pl.ANY)
     mat = (HEADS, D, D)
     scratch = [
+        pltpu.VMEM((ROWS, CH), BF),
+        pltpu.VMEM((ROWS, HEADS * D), BF),
+        pltpu.VMEM((ROWS, HEADS * D), BF),
+        pltpu.VMEM((ROWS, CH), BF),
+        pltpu.SemaphoreType.DMA((5,)),
         pltpu.VMEM((ROWS + 8, CH), F32),
         pltpu.VMEM((ROWS, CH), F32),
         pltpu.VMEM((QK, D, D), F32),
@@ -687,6 +756,8 @@
         pltpu.VMEM(mat, F32),
         pltpu.VMEM((HEADS, PACK, D), BF),
         pltpu.VMEM((HEADS, PACK, D), BF),
+        pltpu.VMEM(mat, BF),
+        pltpu.VMEM(mat, BF),
         pltpu.VMEM(mat, BF),
         pltpu.VMEM(mat, BF),
         pltpu.VMEM(mat, BF),
@@ -718,6 +789,8 @@
         pltpu.SemaphoreType.DMA((BLOCKS,)),
         pltpu.SemaphoreType.DMA((BLOCKS,)),
         pltpu.SemaphoreType.DMA((BLOCKS,)),
+        pltpu.SemaphoreType.DMA((BLOCKS,)),
+        pltpu.SemaphoreType.DMA((BLOCKS,)),
         pltpu.SemaphoreType.DMA((2,)),
         pltpu.SemaphoreType.DMA((2,)),
         pltpu.SemaphoreType.DMA((BLOCKS,)),
@@ -736,8 +809,8 @@
             jax.ShapeDtypeStruct((4, CH), F32),
             jax.ShapeDtypeStruct((2, HEADS), F32),
         ),
-        in_specs=[vmem, vmem, vmem, vmem, pl.BlockSpec(memory_space=pltpu.SMEM), vmem],
-        out_specs=(vmem,) * 5,
+        in_specs=[any_, vmem, vmem, vmem, pl.BlockSpec(memory_space=pltpu.SMEM), any_],
+        out_specs=(any_, any_, vmem, vmem, vmem),
         scratch_shapes=scratch,
         compiler_params=pltpu.CompilerParams(
             collective_id=0, has_side_effects=True, vmem_limit_bytes=56 * 1024 * 1024

time: 80 us -> 74.6 us (0.932)
  Pallas kernels: 79.2 us -> 73.7 us
    pallas_call x1, Pallas kernels: 76.5 us -> 71.1 us  [on_device(): pl.pallas_call(kernel, out_shape=(jax.ShapeDtypeStruct((ROWS, HEADS * D),...]
where the time goes in v4:
time: 74.6 us; the launch traced here: 74.4 us
  Pallas kernels  73.7 us (99%)
    pallas_call x1, Pallas kernels, on_device(): pl.pallas_call(kernel, out_shape=(jax.ShapeDtypeStruct((ROWS, HEADS * D),...  71.1 us
    pallas_call x1, Pallas kernels, hand_on(): pl.pallas_call(hand_on_kernel, out_shape=tuple((jax.ShapeDtypeStruct(a.sh...  2.61 us

profile of v4, /device:TPU:1, one launch (start us, length us, event | category | flops | bytes accessed | tf_op | source)
XLA Modules:
  0.0 74.4 jit_solution(3626059383125240829)
XLA Ops:
  0.6 71.1 %delta_mix.1 = (bf16[128,2048]{1,0:T(8,128)(2,1)}, bf16[128,4096]{1,0:T(8,128)(2,1)}, f32[32,128]{1,0:T(8,128)}, f32[4,4096]{1,0:T(4,128)}, f32[2,16]{1,0:T(2,128)}) custom-call(bf16[128,4096]{1,0:T(8,128)(2,1)} %bitcast.10, f32[4,4096]{1,0:T(4,128)} %w_ref.1, f32[32,128]{1,0:T(8,128)} %bitcast.12, f32[2,16]{1,0:T(2,128)} %hp_ref.1, s32[1,8]{1,0:T(1,128)} %len_ref.1, ...), custom_call_target="tpu_custom_call" | custom-call | tf_op jit(solution)/shard_map/delta_mix/pallas_call | solution.py:803
  71.8 2.6 %hand_on.1 = (bf16[128,2048]{1,0:T(8,128)(2,1)}, bf16[128,4096]{1,0:T(8,128)(2,1)}, f32[32,128]{1,0:T(8,128)}, f32[4,4096]{1,0:T(4,128)}, f32[2,16]{1,0:T(2,128)}) custom-call(bf16[128,2048]{1,0:T(8,128)(2,1)} %get-tuple-element.15.refs_0_, bf16[128,4096]{1,0:T(8,128)(2,1)} %get-tuple-element.16.refs_1_, f32[32,128]{1,0:T(8,128)} %get-tuple-element.17.refs_2_, ...), custom_call_target="tpu_custom_call" | custom-call | tf_op jit(solution)/shard_map/hand_on/pallas_call | solution.py:720

commit v5 on v4

--- a/solution.py
+++ b/solution.py
@@ -1,3 +1,5 @@
+import functools
+
 import jax
 import jax.numpy as jnp
 from jax import lax
@@ -507,11 +509,15 @@
             dm = norms[j] * (dq - q * (D * jnp.sum(q * dq, axis=1, keepdims=True)))
             conv_back(j, group, n, dm)
         dcs[group] = jnp.transpose(packed)[:HG] - jnp.concatenate(colsums, axis=0)
+
+        @pl.when(group > 0)
+        def _():
+            send_piece(group)
         return 0
 
     def backward(step, _):
         group, qk, heads = group_of(step)
-        q_piece, k_piece, v_piece = group, GROUPS + group, 2 * (GROUPS + group)
+        k_piece, v_piece = GROUPS + group, 2 * (GROUPS + group)
         for h in heads:
             @pl.when(h != me)
             def _():
@@ -556,15 +562,9 @@
         rows = jnp.transpose(packed)
         lasts = jnp.concatenate(lasts, axis=0)
         dc = rows[:HG] - jnp.concatenate(colsums, axis=0) + dcs[group]
-        dc = dc + jnp.where(lane[:HG] == D - 1, lasts, 0.0)
-        dg = dot_full(dc, suffix)
-        dz = dg * gts[1, group]
-        bet = gts[2, group]
-        dgo[0, group] = dz
-        dgo[1, group] = rows[HG : 2 * HG] * bet * (1.0 - bet)
-        sums = dot_full(jnp.ones((8, D), F32), jnp.concatenate([dg * gts[0, group], dz], axis=0), 1, 1)
-        red[q_piece, 4:5, 0 : 2 * HG] = sums[0:1]
-        for piece in (q_piece, k_piece, v_piece, v_piece + 1):
+        dgo[0, group] = dc + jnp.where(lane[:HG] == D - 1, lasts, 0.0)
+        dgo[1, group] = rows[HG : 2 * HG]
+        for piece in (k_piece, v_piece, v_piece + 1):
             send_piece(piece)
         return 0
 
@@ -573,6 +573,24 @@
     core_copy = pltpu.make_async_copy(core_ref, core_hbm, io_sem.at[2])
     core_copy.start()
     lax.fori_loop(0, GROUPS, backward, 0)
+
+    def all_groups(ref, which):
+        return jnp.concatenate([ref[which, n] for n in range(GROUPS)], axis=0)
+
+    dg = dot_full(all_groups(dgo, 0), suffix)
+    dz = dg * all_groups(gts, 1)
+    bet = all_groups(gts, 2)
+    sums = dot_full(
+        jnp.ones((8, D), F32), jnp.concatenate([dg * all_groups(gts, 0), dz], axis=0), 1, 1
+    )
+    red[0, 4:5, 0 : 2 * HEADS] = sums[0:1]
+    send_piece(0)
+    dbet = all_groups(dgo, 1) * bet * (1.0 - bet)
+    for n in range(GROUPS):
+        for at, a, b in parts_of(n):
+            lo = n * HG + at
+            dgate_ref[a:b, :] = dz[lo : lo + 2]
+            dgate_ref[HEADS + a : HEADS + b, :] = dbet[lo : lo + 2]
 
     spill = jnp.zeros((8, CH), F32)
     row8w = iota((8, CH), 0)
@@ -637,11 +655,6 @@
 
     mixed_copy(0).start()
 
-    for n in range(GROUPS):
-        for at, a, b in parts_of(n):
-            dgate_ref[a:b, :] = dgo[0, n, at : at + 2]
-            dgate_ref[HEADS + a : HEADS + b, :] = dgo[1, n, at : at + 2]
-
     def wait_dp(i, _):
         other = lax.rem(mine + i, DP)
         dp_copy(other, other).wait_recv()
@@ -691,14 +704,15 @@
 
     lax.fori_loop(1, BLOCKS, wait_all, 0, unroll=True)
     for n in range(GROUPS):
-        sums = r3[n, 4:5]
+        sums = r3[0, 4:5]
         for at, a, b in parts_of(n):
             lo = (at // 2) * D
             dconv_ref[:, a // 2 * D : a // 2 * D + D] = r3[n, 0:4, lo : lo + D]
             dconv_ref[:, (QK + a // 2) * D : (QK + a // 2 + 1) * D] = r3[GROUPS + n, 0:4, lo : lo + D]
             dconv_ref[:, (2 * QK + a) * D : (2 * QK + b) * D] = r3[2 * (GROUPS + n) + at // 2, 0:4]
+            at += n * HG
             dhead_ref[0:1, a:b] = sums[:, at : at + 2]
-            dhead_ref[1:2, a:b] = sums[:, HG + at : HG + at + 2]
+            dhead_ref[1:2, a:b] = sums[:, HEADS + at : HEADS + at + 2]
 
     def drain_all(i, _):
         all_copy(lax.rem(me + i, BLOCKS), me).wait_send()
@@ -710,18 +724,39 @@
     mixed_copy(1).wait()
 
 
-def hand_on_kernel(*refs):
-    n = len(refs) // 2
+def hand_on_kernel(n, *refs):
+    ins, outs, bufs, sems = refs[:n], refs[n : 2 * n], refs[2 * n : 3 * n], refs[3 * n]
+    parts = []
     for i in range(n):
-        refs[n + i][...] = refs[i][...]
+        rows = ins[i].shape[0]
+        size = 32 if rows == ROWS else rows
+        parts += [(i, pl.ds(at, size)) for at in range(0, rows, size)]
+    into = [
+        pltpu.make_async_copy(ins[i].at[at], bufs[i].at[at], sems.at[0, m])
+        for m, (i, at) in enumerate(parts)
+    ]
+    out = [
+        pltpu.make_async_copy(bufs[i].at[at], outs[i].at[at], sems.at[1, m])
+        for m, (i, at) in enumerate(parts)
+    ]
+    for c in into:
+        c.start()
+    for a, b in zip(into, out):
+        a.wait()
+        b.start()
+    for c in out:
+        c.wait()
 
 
 def hand_on(*arrays):
+    n = len(arrays)
     return pl.pallas_call(
-        hand_on_kernel,
+        functools.partial(hand_on_kernel, n),
         out_shape=tuple(jax.ShapeDtypeStruct(a.shape, a.dtype) for a in arrays),
-        in_specs=[pl.BlockSpec(memory_space=pltpu.VMEM)] * len(arrays),
-        out_specs=(pl.BlockSpec(memory_space=pltpu.VMEM),) * len(arrays),
+        in_specs=[pl.BlockSpec(memory_space=pl.ANY)] * n,
+        out_specs=(pl.BlockSpec(memory_space=pl.ANY),) * n,
+        scratch_shapes=[pltpu.VMEM(a.shape, a.dtype) for a in arrays]
+        + [pltpu.SemaphoreType.DMA((2, 16))],
         name="hand_on",
     )(*arrays)
 

time: 74.6 us -> 73.4 us (0.984)
  Pallas kernels: 73.7 us -> 72.5 us
    pallas_call x1, Pallas kernels: 71.1 us -> 70.1 us  [on_device(): pl.pallas_call(kernel, out_shape=(jax.ShapeDtypeStruct((ROWS, HEADS * D),...]
where the time goes in v5:
time: 73.4 us; the launch traced here: 73.2 us
  Pallas kernels  72.5 us (99%)
    pallas_call x1, Pallas kernels, on_device(): pl.pallas_call(kernel, out_shape=(jax.ShapeDtypeStruct((ROWS, HEADS * D),...  70.1 us
    pallas_call x1, Pallas kernels, hand_on(): pl.pallas_call(functools.partial(hand_on_kernel, n), out_shape=tuple((jax...  2.48 us

profile of v5, /device:TPU:1, one launch (start us, length us, event | category | flops | bytes accessed | tf_op | source)
XLA Modules:
  0.0 73.2 jit_solution(12684307729308262916)
XLA Ops:
  0.6 70.1 %delta_mix.1 = (bf16[128,2048]{1,0:T(8,128)(2,1)}, bf16[128,4096]{1,0:T(8,128)(2,1)}, f32[32,128]{1,0:T(8,128)}, f32[4,4096]{1,0:T(4,128)}, f32[2,16]{1,0:T(2,128)}) custom-call(bf16[128,4096]{1,0:T(8,128)(2,1)} %bitcast.10, f32[4,4096]{1,0:T(4,128)} %w_ref.1, f32[32,128]{1,0:T(8,128)} %bitcast.12, f32[2,16]{1,0:T(2,128)} %hp_ref.1, s32[1,8]{1,0:T(1,128)} %len_ref.1, ...), custom_call_target="tpu_custom_call" | custom-call | tf_op jit(solution)/shard_map/delta_mix/pallas_call | solution.py:838
  70.7 2.5 %hand_on.1 = (bf16[128,2048]{1,0:T(8,128)(2,1)}, bf16[128,4096]{1,0:T(8,128)(2,1)}, f32[32,128]{1,0:T(8,128)}, f32[4,4096]{1,0:T(4,128)}, f32[2,16]{1,0:T(2,128)}) custom-call(bf16[128,2048]{1,0:T(8,128)(2,1)} %get-tuple-element.15.refs_0_, bf16[128,4096]{1,0:T(8,128)(2,1)} %get-tuple-element.16.refs_1_, f32[32,128]{1,0:T(8,128)} %get-tuple-element.17.refs_2_, ...), custom_call_target="tpu_custom_call" | custom-call | tf_op jit(solution)/shard_map/hand_on/pallas_call | solution.py:753

commit v6 on v5

--- a/solution.py
+++ b/solution.py
@@ -181,7 +181,7 @@
             slope[:, lanes(block)] = y
         return 0
 
-    lax.fori_loop(0, 8, conv_first, 0)
+    lax.fori_loop(0, 8, conv_first, 0, unroll=2)
 
     def conv(block):
         y = slope[:, lanes(block)]
@@ -645,7 +645,7 @@
             taps_back(4 * step + i)
         return 0
 
-    lax.fori_loop(0, 4, mixed_part, 0)
+    lax.fori_loop(0, 4, mixed_part, 0, unroll=2)
 
     def mixed_copy(half):
         part = pl.ds(half * (CH // 2), CH // 2)
@@ -677,7 +677,7 @@
         return 0
 
     lax.fori_loop(1, BLOCKS, send_all, 0, unroll=True)
-    lax.fori_loop(4, 8, mixed_part, 0)
+    lax.fori_loop(4, 8, mixed_part, 0, unroll=2)
     mixed_copy(1).start()
 
     def drain(i, _):

time: 73.4 us -> 73.8 us (level)
  no operation moved by 1% of the time
where the time goes in v6:
time: 73.8 us; the launch traced here: 73.6 us
  Pallas kernels  72.9 us (99%)
    pallas_call x1, Pallas kernels, on_device(): pl.pallas_call(kernel, out_shape=(jax.ShapeDtypeStruct((ROWS, HEADS * D),...  70.4 us
    pallas_call x1, Pallas kernels, hand_on(): pl.pallas_call(functools.partial(hand_on_kernel, n), out_shape=tuple((jax...  2.48 us

profile of v6, /device:TPU:1, one launch (start us, length us, event | category | flops | bytes accessed | tf_op | source)
XLA Modules:
  0.0 73.6 jit_solution(13839443464626160338)
XLA Ops:
  0.6 70.4 %delta_mix.1 = (bf16[128,2048]{1,0:T(8,128)(2,1)}, bf16[128,4096]{1,0:T(8,128)(2,1)}, f32[32,128]{1,0:T(8,128)}, f32[4,4096]{1,0:T(4,128)}, f32[2,16]{1,0:T(2,128)}) custom-call(bf16[128,4096]{1,0:T(8,128)(2,1)} %bitcast.10, f32[4,4096]{1,0:T(4,128)} %w_ref.1, f32[32,128]{1,0:T(8,128)} %bitcast.12, f32[2,16]{1,0:T(2,128)} %hp_ref.1, s32[1,8]{1,0:T(1,128)} %len_ref.1, ...), custom_call_target="tpu_custom_call" | custom-call | tf_op jit(solution)/shard_map/delta_mix/pallas_call | solution.py:838
  71.1 2.5 %hand_on.1 = (bf16[128,2048]{1,0:T(8,128)(2,1)}, bf16[128,4096]{1,0:T(8,128)(2,1)}, f32[32,128]{1,0:T(8,128)}, f32[4,4096]{1,0:T(4,128)}, f32[2,16]{1,0:T(2,128)}) custom-call(bf16[128,2048]{1,0:T(8,128)(2,1)} %get-tuple-element.15.refs_0_, bf16[128,4096]{1,0:T(8,128)(2,1)} %get-tuple-element.16.refs_1_, f32[32,128]{1,0:T(8,128)} %get-tuple-element.17.refs_2_, ...), custom_call_target="tpu_custom_call" | custom-call | tf_op jit(solution)/shard_map/hand_on/pallas_call | solution.py:753
